TPU v7x, 256 devices: a whole 4x4x8 slice. The times are simulated.
256 devices in a mesh: side: 2 (over core), group: 4 (over x), dev: 32 (over y, z).
Axes of the slice: x: 4, y: 4, z: 8, core: 2. Of those that a mesh axis runs over, the one named last changes fastest.
Arguments:
- embeds: bfloat16 [2, 1536, 256, 256], P('side', ('group', 'dev')), may hold values from -0.5 to 0.5
- log_weights: float32 [2, 1536, 256], P('side', ('group', 'dev')), may hold values from -4 to 4
- listing: int32 [2, 7680, 2], P('side', ('group', 'dev')), may hold values from 0 to 1535, as said below
Outputs:
- potential: float32 [2, 1536, 256], P('side', ('group', 'dev'))
Inputs may be any that keep to these rules, and one draw needn't show every extreme that they name: Block b of a side lies on device b // 12 of that side (group+dev order). Device e of side s holds in listing[s] exactly the 60 pairs whose side-s block lies on it; listing[1] holds the pairs of listing[0] with the two ids swapped, each once. Every block of either side is in 2 or 8 listed pairs. The pairs between the blocks of one device and the blocks of one device of the other side number at most 1, and every device has such a partner device with exactly 1.
All inputs are finite; a program needn't handle non-finite values.
Results may differ from a plain program's by a relative error of at most 0.0003.
Values may be sent and summed in bfloat16 or wider, within the bound.
A program may use at most 128 MiB of HBM per device.

v0:
```python
import jax
import jax.numpy as jnp
from jax import lax
from jax.sharding import PartitionSpec as P

MOST = 8
ITERS = 3


entropic_blur = 0.1


def swapped(block, axis, bit):
    count = lax.axis_size(axis)
    route = []
    for low in range(count):
        high = low | 1 << bit
        if high != low and high < count:
            route += [(low, high), (high, low)]
    return lax.ppermute(block, axis, route)


def select_rows(hot, table):
    flat = table.reshape(table.shape[0], -1)
    picked = jnp.dot(
        hot.astype(table.dtype),
        flat,
        preferred_element_type=jnp.float32,
        precision=lax.Precision.HIGHEST,
    )
    return picked.astype(table.dtype).reshape((hot.shape[0],) + table.shape[1:])


def per_device(embeds, log_weights, listing):
    own_blocks = embeds[0]
    own_weight = log_weights[0]
    pair_table = listing[0]
    block_count = own_blocks.shape[0]
    row_count = own_blocks.shape[1]
    width_count = own_blocks.shape[2]
    group_count = lax.axis_size("group")
    member_count = lax.axis_size("dev")
    peer_count = group_count * member_count
    pair_count = pair_table.shape[0]
    capacity = (pair_count + peer_count - 1) // peer_count
    slot_total = peer_count * capacity
    position = lax.axis_index("group") * member_count + lax.axis_index("dev")
    own_local = pair_table[:, 0] - position * block_count
    owner_dev = pair_table[:, 1] // block_count
    far_local = pair_table[:, 1] % block_count
    owner_hot = (owner_dev[:, None] == jnp.arange(peer_count)[None, :]).astype(jnp.int32)
    earlier = jnp.cumsum(owner_hot, axis=0) - owner_hot
    slot_rank = jnp.sum(earlier * owner_hot, axis=1)
    slot_index = owner_dev * capacity + slot_rank
    slot_hot = slot_index[:, None] == jnp.arange(slot_total)[None, :]
    wanted = jnp.sum(jnp.where(slot_hot, far_local[:, None], 0), axis=0)
    requests = lax.all_to_all(wanted, ("group", "dev"), split_axis=0, concat_axis=0, tiled=True)
    request_hot = requests[:, None] == jnp.arange(block_count)[None, :]
    mirror = swapped(own_blocks, "side", 0)
    outgoing = select_rows(request_hot, mirror)
    routed = lax.all_to_all(outgoing, ("group", "dev"), split_axis=0, concat_axis=0, tiled=True)
    far_sq = jnp.sum(jnp.square(routed.astype(jnp.float32)), axis=2)
    own_sq = jnp.sum(jnp.square(own_blocks.astype(jnp.float32)), axis=2)
    block_hot = (own_local[:, None] == jnp.arange(block_count)[None, :]).astype(jnp.int32)
    block_rank = jnp.sum((jnp.cumsum(block_hot, axis=0) - block_hot) * block_hot, axis=1)
    cell_index = own_local * MOST + block_rank
    cell_hot = cell_index[:, None] == jnp.arange(block_count * MOST)[None, :]
    pair_slot = jnp.sum(jnp.where(cell_hot, slot_index[:, None], 0), axis=0)
    filled = jnp.any(cell_hot, axis=0)
    cell_slot_hot = jnp.logical_and(
        pair_slot[:, None] == jnp.arange(slot_total)[None, :], filled[:, None]
    )
    cell_far = select_rows(cell_slot_hot, routed).reshape(block_count, MOST, row_count, width_count)
    cell_far_sq = select_rows(cell_slot_hot, far_sq).reshape(block_count, MOST, row_count)
    live_cells = filled.reshape(block_count, MOST)
    potential = jnp.zeros(own_weight.shape, jnp.float32)
    for iteration in range(ITERS):
        shifted = potential + own_weight
        mirror_level = swapped(shifted, "side", 0)
        send_level = select_rows(request_hot, mirror_level)
        far_level = lax.all_to_all(
            send_level, ("group", "dev"), split_axis=0, concat_axis=0, tiled=True
        )
        cell_level = select_rows(cell_slot_hot, far_level).reshape(block_count, MOST, row_count)

        def block_pass(inputs):
            block_rows, block_sq, far_rows, far_norm, far_shift, live_mask = inputs
            cross_term = jnp.einsum(
                "id,mjd->imj", block_rows, far_rows, preferred_element_type=jnp.float32
            )
            pair_cost = block_sq[:, None, None] + far_norm[None] - 2.0 * cross_term
            scores = jnp.where(
                live_mask[None, :, None], far_shift[None] - pair_cost / entropic_blur, -jnp.inf
            )
            row_top = jnp.max(scores, axis=(1, 2))
            row_total = jnp.sum(jnp.exp(scores - row_top[:, None, None]), axis=(1, 2))
            return -(row_top + jnp.log(row_total))

        transport = lax.map(
            block_pass, (own_blocks, own_sq, cell_far, cell_far_sq, cell_level, live_cells)
        )
        potential = 0.5 * (potential + transport)
    return potential[None]


def solution(mesh):
    placed = (
        P("side", ("group", "dev"), None, None),
        P("side", ("group", "dev"), None),
        P("side", ("group", "dev"), None),
    )
    return jax.shard_map(
        per_device,
        mesh=mesh,
        in_specs=placed,
        out_specs=P("side", ("group", "dev"), None),
        check_vma=False,
    )
```

profile of v0, /device:TPU:1, one launch (start us, length us, event | category | flops | bytes accessed | tf_op | source)
XLA Modules:
  0.0 621.0 jit_solution(1945464747050710858)
XLA Ops:
  0.0 3.2 collective-permute-start.1
  5.3 24.1 %all_to_all.50 = s32[128,1,1]{2,1,0:T(1,128)S(1)} all-to-all(s32[128,1,1]{2,1,0:T(1,128)S(1)} %copy.24), channel_id=1, replica_groups=mesh['side'=2,'group'=4,'dev'=32] {'group','dev'}, dimensions={0} | all-to-all | bytes 1024 | tf_op jit(solution)/shard_map/all_to_all | solution.py:57
  29.4 2.3 reduce
  32.8 6.2 all-to-all-start.1
  40.4 4.8 convolution_convert_fusion
  45.2 7.8 %copy.36 = bf16[16,8,256,256]{3,2,1,0:T(8,128)(2,1)} copy(bf16[16,8,256,256]{3,1,2,0:T(8,128)(2,1)S(1)} %bitcast.160) | data formatting | bytes 33554432
  53.0 13.9 %all-to-all-start.2 = ((bf16[128,256,256]{2,1,0:T(8,128)(2,1)}), bf16[128,256,256]{2,1,0:T(8,128)(2,1)}, u32[]{:S(2)}, u32[]{:S(2)}) async-start(bf16[128,256,256]{2,1,0:T(8,128)(2,1)} %bitcast.159), calls=%async_computation.2 | async-start | bytes 33554432 | tf_op jit(solution)/shard_map/all_to_all | solution.py:61
  68.4 362.7 %all-to-all-done.2 = bf16[128,256,256]{2,1,0:T(8,128)(2,1)} async-done(((bf16[128,256,256]{2,1,0:T(8,128)(2,1)}), bf16[128,256,256]{2,1,0:T(8,128)(2,1)}, u32[]{:S(2)}, u32[]{:S(2)}) %all-to-all-start.2) | async-done | bytes 16777248 | tf_op jit(solution)/shard_map/all_to_all | solution.py:61
  431.1 7.6 %multiply_reduce_fusion = f32[128,256]{1,0:T(8,128)S(1)} fusion(bf16[128,256,256]{2,1,0:T(8,128)(2,1)} %all-to-all-done.2), kind=kLoop, calls=%fused_computation.38 | loop fusion | flops 25133056 | bytes 16908288 | tf_op jit(solution)/shard_map/reduce_sum | solution.py:62
  439.0 17.9 %copy.37 = bf16[16,8,256,256]{3,1,2,0:T(8,128)(2,1)} copy(bf16[16,8,256,256]{3,2,1,0:T(8,128)(2,1)} %bitcast.49) | data formatting | bytes 33554432
  456.8 13.7 %convolution_convert_fusion.1 = bf16[96,65536]{1,0:T(8,128)(2,1)} fusion(bf16[128,65536]{1,0:T(8,128)(2,1)} %bitcast.157, s32[96]{0:T(128)S(1)} %select_reduce_fusion.1, pred[96]{0:T(512)(128)(4,1)S(1)} %fusion.40), kind=kOutput, calls=%fused_computation.37 | convolution fusion | flops 1616928768 | bytes 29360608 | tf_op jit(solution)/shard_map/dot_general | solution.py:25
  470.5 11.9 %copy.26 = bf16[12,8,256,256]{3,2,1,0:T(8,128)(2,1)} copy(bf16[12,8,256,256]{3,1,2,0:T(8,128)(2,1)} %bitcast.158) | data formatting | bytes 25165824 | tf_op jit(solution)/shard_map/while | solution.py:99
  482.4 30.1 %while.30 = (s32[]{:T(128)}, f32[12,256]{1,0:T(8,128)S(1)}, pred[12,8]{1,0:T(8,128)(4,1)S(1)}, f32[12,8,256]{2,1,0:T(8,128)S(1)}, f32[12,256]{1,0:T(8,128)S(1)},...) while((s32[]{:T(128)}, f32[12,256]{1,0:T(8,128)S(1)}, ...), condition=%wide.region_12.13_spmd, body=%wide.region_9.12_spmd.sunk | while | flops 273154048 | bytes 5436037 | solution.py:99
  490.0 2.0 fusion.68
  502.6 2.0 fusion.68
  512.6 5.6 collective-permute-start.2
  520.1 6.4 %all-to-all-start.3 = ((f32[128,1,256]{2,1,0:T(1,128)}), f32[128,1,256]{2,1,0:T(1,128)S(1)}, u32[]{:S(2)}, u32[]{:S(2)}) async-start(f32[128,1,256]{2,1,0:T(1,128)} %copy.27), calls=%async_computation.3 | async-start | bytes 262144 | tf_op jit(solution)/shard_map/all_to_all | solution.py:81
  526.5 11.8 %all-to-all-done.3 = f32[128,1,256]{2,1,0:T(1,128)S(1)} async-done(((f32[128,1,256]{2,1,0:T(1,128)}), f32[128,1,256]{2,1,0:T(1,128)S(1)}, u32[]{:S(2)}, u32[]{:S(2)}) %all-to-all-start.3) | async-done | bytes 131104 | tf_op jit(solution)/shard_map/all_to_all | solution.py:81
  538.5 30.2 %while.31 = (s32[]{:T(128)}, f32[12,256]{1,0:T(8,128)S(1)}, pred[12,8]{1,0:T(8,128)(4,1)S(1)}, f32[12,8,256]{2,1,0:T(8,128)S(1)}, f32[12,256]{1,0:T(8,128)S(1)},...) while((s32[]{:T(128)}, f32[12,256]{1,0:T(8,128)S(1)}, ...), condition=%wide.region_16.17_spmd, body=%wide.region_13.16_spmd.sunk | while | flops 273154048 | bytes 5436037 | solution.py:99
  551.1 2.0 fusion.69
  563.7 2.0 fusion.69
  572.1 6.2 all-to-all-start.4
  578.3 11.8 %all-to-all-done.4 = f32[128,1,256]{2,1,0:T(1,128)S(1)} async-done(((f32[128,1,256]{2,1,0:T(1,128)}), f32[128,1,256]{2,1,0:T(1,128)S(1)}, u32[]{:S(2)}, u32[]{:S(2)}) %all-to-all-start.4) | async-done | bytes 131104 | tf_op jit(solution)/shard_map/all_to_all | solution.py:81
  590.3 30.1 %while.32 = (s32[]{:T(128)}, f32[12,256]{1,0:T(8,128)S(1)}, pred[12,8]{1,0:T(8,128)(4,1)S(1)}, f32[12,8,256]{2,1,0:T(8,128)S(1)}, f32[12,256]{1,0:T(8,128)S(1)},...) while((s32[]{:T(128)}, f32[12,256]{1,0:T(8,128)S(1)}, ...), condition=%wide.region_20.21_spmd, body=%wide.region_17.20_spmd.sunk | while | flops 273154048 | bytes 5436037 | solution.py:99
  (297 shorter events, 93.1 us)
Async XLA Ops:
  0.0 39.0 %collective-permute-start.1 = (bf16[12,256,256]{2,1,0:T(8,128)(2,1)}, bf16[12,256,256]{2,1,0:T(8,128)(2,1)S(1)}, u32[]{:S(2)}, u32[]{:S(2)}) collective-permute-start(bf16[12,256,256]{2,1,0:T(8,128)(2,1)} %bitcast.163), channel_id=1, source_target_pairs={{0,128},{128,0},{1,129},{129,1},{2,130},{130,2},{3,131},{131,3},{4... | collective-permute-start | bytes 4718600 | tf_op jit(solution)/shard_map/ppermute | solution.py:20
  4.0 27.8 %collective-permute-start = (f32[12,256]{1,0:T(8,128)S(1)}, f32[12,256]{1,0:T(8,128)S(1)}, u32[]{:S(2)}, u32[]{:S(2)}) collective-permute-start(f32[12,256]{1,0:T(8,128)S(1)} %bitcast.171), channel_id=1, source_target_pairs={{0,128},{128,0},{1,129},{129,1},{2,130},{130,2},{3,131},{131,3},{4... | collective-permute-start | bytes 36872 | tf_op jit(solution)/shard_map/ppermute | solution.py:20
  32.8 20.2 %all-to-all-start.1 = ((f32[128,1,256]{2,1,0:T(1,128)}), f32[128,1,256]{2,1,0:T(1,128)S(1)}, u32[]{:S(2)}, u32[]{:S(2)}) async-start(f32[128,1,256]{2,1,0:T(1,128)} %copy.25), calls=%async_computation.1 | async-start | bytes 262144 | tf_op jit(solution)/shard_map/all_to_all | solution.py:81
  53.0 14.3 %copy-start.2 = (s32[1,60,2]{1,2,0:T(2,128)S(1)}, s32[1,60,2]{1,2,0:T(2,128)}, u32[]{:S(2)}) copy-start(s32[1,60,2]{1,2,0:T(2,128)} %param.11) | copy-start | bytes 1444
  53.0 14.7 %copy-start = (bf16[1,12,256,256]{3,2,1,0:T(8,128)(2,1)S(1)}, bf16[1,12,256,256]{3,2,1,0:T(8,128)(2,1)}, u32[]{:S(2)}) copy-start(bf16[1,12,256,256]{3,2,1,0:T(8,128)(2,1)} %param.9) | copy-start | bytes 4718596
  53.0 378.1 %all-to-all-start.2 = ((bf16[128,256,256]{2,1,0:T(8,128)(2,1)}), bf16[128,256,256]{2,1,0:T(8,128)(2,1)}, u32[]{:S(2)}, u32[]{:S(2)}) async-start(bf16[128,256,256]{2,1,0:T(8,128)(2,1)} %bitcast.159), calls=%async_computation.2 | async-start | bytes 33554432 | tf_op jit(solution)/shard_map/all_to_all | solution.py:61
  482.4 30.1 %copy-start.1 = (f32[1,12,256]{2,0,1:T(1,128)S(1)}, f32[1,12,256]{2,0,1:T(1,128)}, u32[]{:S(2)}) copy-start(f32[1,12,256]{2,0,1:T(1,128)} %param.10) | copy-start | bytes 36868
  512.6 6.5 %collective-permute-start.2 = (f32[12,256]{1,0:T(8,128)S(1)}, f32[12,256]{1,0:T(8,128)S(1)}, u32[]{:S(2)}, u32[]{:S(2)}) collective-permute-start(f32[12,256]{1,0:T(8,128)S(1)} %multiply_add_fusion), channel_id=1, source_target_pairs={{0,128},{128,0},{1,129},{129,1},{2,130},{130,2},{3,131},{131,3},{4... | collective-permute-start | bytes 36872 | tf_op jit(solution)/shard_map/ppermute | solution.py:20
  520.1 18.1 %all-to-all-start.3 = ((f32[128,1,256]{2,1,0:T(1,128)}), f32[128,1,256]{2,1,0:T(1,128)S(1)}, u32[]{:S(2)}, u32[]{:S(2)}) async-start(f32[128,1,256]{2,1,0:T(1,128)} %copy.27), calls=%async_computation.3 | async-start | bytes 262144 | tf_op jit(solution)/shard_map/all_to_all | solution.py:81
  568.7 2.4 collective-permute-start.3
  572.1 17.9 %all-to-all-start.4 = ((f32[128,1,256]{2,1,0:T(1,128)}), f32[128,1,256]{2,1,0:T(1,128)S(1)}, u32[]{:S(2)}, u32[]{:S(2)}) async-start(f32[128,1,256]{2,1,0:T(1,128)} %copy.29), calls=%async_computation.4 | async-start | bytes 262144 | tf_op jit(solution)/shard_map/all_to_all | solution.py:81
where the time goes:
time: 623 us; the launch traced here: 621 us
  waiting for transfers between devices  388 us (62%)
  matrix products  92.9 us (15%)
  local copies, waits for them, and re-layouts  45.5 us (7%)
  starting transfers between devices  43 us (7%)
  other arithmetic  25.5 us (4%)
  blocking collectives  24.1 us (4%)
    all_to_all x1, waiting for transfers between devices, per_device(): lax.all_to_all(outgoing, ('group', 'dev'), split_axis=0, concat_axis=0, t...  363 us
    dot_general x36, matrix products, block_pass(): jnp.einsum('id,mjd->imj', block_rows, far_rows, preferred_element_type=jn...  72.7 us
    unnamed x11, local copies, waits for them, and re-layouts  27.8 us
    all_to_all x1, blocking collectives, per_device(): lax.all_to_all(wanted, ('group', 'dev'), split_axis=0, concat_axis=0, til...  24.1 us
    all_to_all x3, waiting for transfers between devices, per_device(): lax.all_to_all(send_level, ('group', 'dev'), split_axis=0, concat_axis=0,...  23.5 us
    dot_general x9, matrix products, select_rows(): jnp.dot(hot.astype(table.dtype), flat, preferred_element_type=jnp.float32...  20.2 us
    all_to_all x3, starting transfers between devices, per_device(): lax.all_to_all(send_level, ('group', 'dev'), split_axis=0, concat_axis=0,...  18.7 us
    all_to_all x1, starting transfers between devices, per_device(): lax.all_to_all(outgoing, ('group', 'dev'), split_axis=0, concat_axis=0, t...  13.9 us
  transfers between devices with their start and end apart: 8, of which 5 were waited for; matrix products, arithmetic and copies ran while one was open for 3% of the time, Pallas kernels for 0%

commit v1 on v0

v1 whole, which is shorter than its diff:
```python
import functools
import math

import jax
import jax.numpy as jnp
from jax import lax
from jax.experimental import pallas as pl
from jax.experimental.pallas import tpu as pltpu
from jax.sharding import PartitionSpec as P

MESH = pl.DeviceIdType.MESH
ITERS = 3
NX, NY, NZ = 4, 4, 8
LOG2E = math.log2(math.e)
LN2 = math.log(2.0)
INV_BLUR = 10.0
SCALE = 2.0 * INV_BLUR * LOG2E
EMPTY = -1e30
VMEM_CAP = 48 * 1024 * 1024


def where(pred, a, b):
    return jnp.where(pred, a, b)


class Place:
    def __init__(self):
        self.k = lax.axis_index("side")
        self.x = lax.axis_index("group")
        dev = lax.axis_index("dev")
        self.y = dev // NZ
        self.z = dev % NZ
        self.kq = (self.x + self.y) % 2
        self.own_slot = self.y * 2 + self.x // 2

    def dev(self, k, x, y, z):
        return (k, x, y * NZ + z)

    def owner(self, j):
        if j < 8:
            return self.dev(jnp.int32(0), self.x, self.y, jnp.int32(j)), jnp.logical_and(self.k == 0, self.z == j)
        d = j - 8
        y0 = d // 2
        x0 = 2 * (d % 2) + (y0 + self.k) % 2
        me = jnp.logical_and(self.k == 1, jnp.logical_and(self.x == x0, self.y == y0))
        return self.dev(jnp.int32(1), x0, jnp.int32(y0), self.z), me

    def meeter(self, j):
        src = self.k == 0
        kk = where(src, j % 2, self.kq)
        xx = where(src, self.x, j % 4)
        yy = where(src, self.y, j // 4)
        zz = where(src, j // 2, self.z)
        me = jnp.logical_and(
            jnp.logical_and(kk == self.k, xx == self.x), jnp.logical_and(yy == self.y, zz == self.z)
        )
        return self.dev(kk, xx, yy, zz), me

    def peers(self):
        return 16 - where(jnp.logical_or(self.k == 0, self.kq == 1), 1, 0)

    def level_slot(self):
        return where(self.k == 0, self.z, 8 + self.own_slot)

    def meet_slot(self, j):
        return self.z * 2 + self.k if j < 8 else self.y * 4 + self.x


def remote(src, dst, send_sem, recv_sem, device):
    return pltpu.make_async_remote_copy(
        src_ref=src, dst_ref=dst, send_sem=send_sem, recv_sem=recv_sem, device_id=device, device_id_type=MESH
    )


def spread_start(pc, level, table, send_sem, recv_sem):
    slot = pc.level_slot()
    for j in range(16):
        device, me = pc.meeter(j)

        @pl.when(jnp.logical_not(me))
        def _():
            remote(level, table.at[slot], send_sem.at[j], recv_sem.at[slot], device).start()

        @pl.when(me)
        def _():
            table[slot] = level[...]


def spread_wait(pc, level, table, send_sem, recv_sem):
    for j in range(16):
        device, me = pc.meeter(j)
        owner, mine = pc.owner(j)

        @pl.when(jnp.logical_not(mine))
        def _():
            remote(level, table.at[j], send_sem.at[j], recv_sem.at[j], owner).wait_recv()

    for j in range(16):
        device, me = pc.meeter(j)

        @pl.when(jnp.logical_not(me))
        def _():
            remote(level, table.at[j], send_sem.at[j], recv_sem.at[j], device).wait_send()


def signal(sem, device):
    pl.semaphore_signal(sem, inc=1, device_id=device, device_id_type=MESH)


def gather_kernel(
    emb, level, src_out, tgt_out, level_out, list_out,
    table, local_sem, own_sem, z_send, z_recv, sib_send, sib_recv,
    first_send, first_recv, next_send, next_recv, relay_send, relay_recv, lv_send, lv_recv,
):
    pc = Place()
    k, x, y, z = pc.k, pc.x, pc.y, pc.z
    sibling = pc.dev(1 - k, x, y, z)
    zdev = [pc.dev(k, x, y, (z + 1) % NZ), pc.dev(k, x, y, (z + NZ - 1) % NZ)]
    xdev = [pc.dev(k, (x + 1) % NX, y, z), pc.dev(k, (x + NX - 1) % NX, y, z)]
    ydev = [pc.dev(k, x, (y + 1) % NY, z), pc.dev(k, x, (y + NY - 1) % NY, z)]

    barrier = pltpu.get_barrier_semaphore()
    for device in [sibling] + zdev + xdev + ydev:
        signal(barrier, device)
    for j in range(16):
        device, mine = pc.owner(j)

        @pl.when(jnp.logical_not(mine))
        def _():
            signal(barrier, device)

    pl.semaphore_wait(barrier, 7 + pc.peers())

    native = k == pc.kq

    def src_at(h, z0, s):
        return src_out.at[h, z0, pl.ds(3 * s, 3)]

    def tgt_at(f, line, o, s):
        return tgt_out.at[f, line, o, pl.ds(3 * s, 3)]

    line_of = [y, x]
    spot_of = [x, y]
    spread_dev = [xdev, ydev]
    onward_dev = [ydev, xdev]

    @pl.when(k == 0)
    def _():
        for h in (1, 0):
            for s in range(2):
                part = emb.at[pl.ds(6 * h + 3 * s, 3)]
                remote(part, src_at(h, z, s), own_sem.at[0, h, s], own_sem.at[1, h, s], sibling).start()
        for h in range(2):
            for s in range(2):
                part = emb.at[pl.ds(6 * h + 3 * s, 3)]
                pltpu.make_async_copy(part, src_at(h, z, s), local_sem.at[h, s]).start()

    @pl.when(jnp.logical_and(k == 1, pc.kq == 1))
    def _():
        for f in range(2):
            for s in range(2):
                part = emb.at[pl.ds(6 * f + 3 * s, 3)]
                pltpu.make_async_copy(part, tgt_at(f, line_of[f], spot_of[f] // 2, s), local_sem.at[f, s]).start()

    @pl.when(jnp.logical_and(k == 1, pc.kq == 0))
    def _():
        for f in range(2):
            for s in range(2):
                part = emb.at[pl.ds(6 * f + 3 * s, 3)]
                remote(
                    part, tgt_at(f, line_of[f], spot_of[f] // 2, s), own_sem.at[0, f, s], own_sem.at[1, f, s], sibling
                ).start()

    spread_start(pc, level, table, lv_send, lv_recv)

    def z_copy(way, r, s):
        z0 = (z - r + NZ) % NZ if way == 0 else (z + r) % NZ
        part = src_out.at[k, z0, pl.ds(3 * s, 3)]
        return remote(part, part, z_send.at[way, r, s], z_recv.at[way, r, s], zdev[way])

    def z_landed(way, r, s):
        z0 = (z - r - 1 + NZ) % NZ if way == 0 else (z + r + 1) % NZ
        part = src_out.at[k, z0, pl.ds(3 * s, 3)]
        return remote(part, part, z_send.at[way, r, s], z_recv.at[way, r, s], zdev[way])

    def sib_copy(way, r, s):
        z0 = (z - r - 1 + NZ) % NZ if way == 0 else (z + r + 1) % NZ
        part = src_out.at[k, z0, pl.ds(3 * s, 3)]
        return remote(part, part, sib_send.at[way, r, s], sib_recv.at[way, r, s], sibling)

    def sib_landed(way, r, s):
        z0 = (z - r - 1 + NZ) % NZ if way == 0 else (z + r + 1) % NZ
        part = src_out.at[1 - k, z0, pl.ds(3 * s, 3)]
        return remote(part, part, sib_send.at[way, r, s], sib_recv.at[way, r, s], sibling)

    def z_subs(way, r):
        return (0, 1) if r < 3 else (way,)

    for s in range(2):
        @pl.when(k == 0)
        def _():
            part = emb.at[pl.ds(3 * s, 3)]
            pltpu.make_async_copy(part, src_at(0, z, s), local_sem.at[0, s]).wait()

        @pl.when(k == 1)
        def _():
            part = src_at(1, z, s)
            remote(part, part, own_sem.at[0, 1, s], own_sem.at[1, 1, s], sibling).wait_recv()

        for way in range(2):
            z_copy(way, 0, s).start()

    def first_copy(f, way, o, s):
        part = tgt_at(f, line_of[f], o, s)
        return remote(part, part, first_send.at[f, way, s], first_recv.at[f, way, s], spread_dev[f][way])

    def next_copy(f, way, o, s):
        part = tgt_at(f, line_of[f], o, s)
        return remote(part, part, next_send.at[f, way, o, s], next_recv.at[f, way, o, s], onward_dev[f][way])

    def from_line(f, way):
        n = line_of[f]
        return (n + 3) % 4 if way == 0 else (n + 1) % 4

    def next_landed(f, way, o, s):
        part = tgt_at(f, from_line(f, way), o, s)
        return remote(part, part, next_send.at[f, way, o, s], next_recv.at[f, way, o, s], onward_dev[f][way])

    def relay_copy(f, way, o):
        part = tgt_at(f, from_line(f, way), o, way)
        return remote(part, part, relay_send.at[f, way, o], relay_recv.at[f, way, o], onward_dev[f][way])

    def relay_landed(f, way, o):
        part = tgt_at(f, (line_of[f] + 2) % 4, o, way)
        return remote(part, part, relay_send.at[f, way, o], relay_recv.at[f, way, o], onward_dev[f][way])

    home = [spot_of[f] // 2 for f in range(2)]
    near = [[((spot_of[f] + 3) % 4) // 2, ((spot_of[f] + 1) % 4) // 2] for f in range(2)]

    @pl.when(native)
    def _():
        for s in range(2):
            for f in range(2):
                part = tgt_at(f, line_of[f], home[f], s)

                @pl.when(k == 1)
                def _():
                    pltpu.make_async_copy(emb.at[pl.ds(6 * f + 3 * s, 3)], part, local_sem.at[f, s]).wait()

                @pl.when(k == 0)
                def _():
                    remote(part, part, own_sem.at[0, f, s], own_sem.at[1, f, s], sibling).wait_recv()

                for way in range(2):
                    first_copy(f, way, home[f], s).start()
        for s in range(2):
            for f in range(2):
                for way in range(2):
                    next_copy(f, way, home[f], s).start()

    def z_forward(r):
        for s in range(2):
            for way in range(2):
                if s in z_subs(way, r):
                    z_landed(way, r, s).wait_recv()
                    if r < 3 and s in z_subs(way, r + 1):
                        z_copy(way, r + 1, s).start()
                    sib_copy(way, r, s).start()

    z_forward(0)

    @pl.when(jnp.logical_not(native))
    def _():
        for s in range(2):
            for f in range(2):
                for way in range(2):
                    o = near[f][way]
                    first_copy(f, way, o, s).wait_recv()
                    if s == way:
                        first_copy(f, way, o, s).start()
                    for w in range(2):
                        next_copy(f, w, o, s).start()

    z_forward(1)

    @pl.when(native)
    def _():
        for f in range(2):
            for way in range(2):
                o = 1 - home[f]
                first_copy(f, way, o, way).wait_recv()
                for w in range(2):
                    next_copy(f, w, o, way).start()

    def onward(nth):
        for s in range(2):
            for f in range(2):
                o = home[f] if nth == 0 else 1 - home[f]
                for way in range(2):
                    next_landed(f, way, o, s).wait_recv()
                    if s == way:
                        relay_copy(f, way, o).start()

    onward(0)
    z_forward(2)
    onward(1)
    z_forward(3)

    spread_wait(pc, level, table, lv_send, lv_recv)
    level_out[...] = table[...]
    codes = table[0:8, 12, 0:128]
    low = ((z * 2 + k) * 2048).astype(jnp.float32)
    mine = jnp.logical_and(codes >= low, codes < low + 2048.0)
    hit = jnp.where(mine, 1.0, 0.0)
    row_id = lax.broadcasted_iota(jnp.int32, (128, 128), 0)
    col_id = lax.broadcasted_iota(jnp.int32, (128, 128), 1)
    upper = jnp.where(row_id < col_id, 1.0, 0.0)
    within = jnp.dot(hit, upper, preferred_element_type=jnp.float32)
    totals = jnp.broadcast_to(jnp.sum(hit, axis=1, keepdims=True), (8, 128))
    below = jnp.where(
        lax.broadcasted_iota(jnp.int32, (8, 8), 1) < lax.broadcasted_iota(jnp.int32, (8, 8), 0), 1.0, 0.0
    )
    before = jnp.dot(below, totals, preferred_element_type=jnp.float32, precision=lax.Precision.HIGHEST)
    rank = jnp.where(mine, within + before, -1.0)
    packed = codes - low + 2048.0 * lax.broadcasted_iota(jnp.int32, (8, 128), 0).astype(jnp.float32)
    want = row_id.astype(jnp.float32)
    picked = jnp.zeros((128, 128), jnp.float32)
    for r in range(8):
        picked = picked + jnp.where(want == rank[r : r + 1, :], packed[r : r + 1, :], 0.0)
    entries = jnp.broadcast_to(jnp.sum(picked, axis=1, keepdims=True), (128, 128))
    line = jnp.sum(jnp.where(row_id == col_id, entries, 0.0), axis=0, keepdims=True)
    count = jnp.broadcast_to(jnp.sum(totals[:, 0:1], axis=0, keepdims=True), (1, 128))
    list_out[...] = jnp.concatenate([line, count, jnp.zeros((6, 128), jnp.float32)], axis=0).astype(jnp.int32)

    for f in range(2):
        for way in range(2):
            for o in range(2):
                relay_landed(f, way, o).wait_recv()
    for r in range(4):
        for way in range(2):
            for s in z_subs(way, r):
                sib_landed(way, r, s).wait_recv()

    @pl.when(k == 1)
    def _():
        for s in range(2):
            part = src_at(0, z, s)
            remote(part, part, own_sem.at[0, 0, s], own_sem.at[1, 0, s], sibling).wait_recv()

    @pl.when(k == 0)
    def _():
        for s in range(2):
            part = emb.at[pl.ds(6 + 3 * s, 3)]
            pltpu.make_async_copy(part, src_at(1, z, s), local_sem.at[1, s]).wait()
        for h in range(2):
            for s in range(2):
                part = emb.at[pl.ds(6 * h + 3 * s, 3)]
                remote(part, src_at(h, z, s), own_sem.at[0, h, s], own_sem.at[1, h, s], sibling).wait_send()

    @pl.when(jnp.logical_and(k == 1, pc.kq == 0))
    def _():
        for f in range(2):
            for s in range(2):
                part = emb.at[pl.ds(6 * f + 3 * s, 3)]
                remote(
                    part, tgt_at(f, line_of[f], home[f], s), own_sem.at[0, f, s], own_sem.at[1, f, s], sibling
                ).wait_send()

    for r in range(4):
        for way in range(2):
            for s in z_subs(way, r):
                z_copy(way, r, s).wait_send()
                sib_copy(way, r, s).wait_send()
    for f in range(2):
        for way in range(2):
            for s in range(2):
                @pl.when(native)
                def _():
                    first_copy(f, way, home[f], s).wait_send()

            @pl.when(jnp.logical_not(native))
            def _():
                first_copy(f, way, near[f][way], way).wait_send()

            for o in range(2):
                relay_copy(f, way, o).wait_send()
                for s in range(2):
                    next_copy(f, way, o, s).wait_send()


def gather(emb, level):
    DMA = pltpu.SemaphoreType.DMA
    any_spec = pl.BlockSpec(memory_space=pl.ANY)
    vmem = pl.BlockSpec(memory_space=pltpu.VMEM)
    return pl.pallas_call(
        gather_kernel,
        out_shape=(
            jax.ShapeDtypeStruct((2, 8, 6, 256, 256), jnp.bfloat16),
            jax.ShapeDtypeStruct((2, 4, 2, 6, 256, 256), jnp.bfloat16),
            jax.ShapeDtypeStruct((16, 16, 256), jnp.float32),
            jax.ShapeDtypeStruct((8, 128), jnp.int32),
        ),
        in_specs=[any_spec, vmem],
        out_specs=(any_spec, any_spec, vmem, vmem),
        scratch_shapes=[
            pltpu.VMEM((16, 16, 256), jnp.float32),
            DMA((2, 2)),
            DMA((2, 2, 2)),
            DMA((2, 4, 2)),
            DMA((2, 4, 2)),
            DMA((2, 4, 2)),
            DMA((2, 4, 2)),
            DMA((2, 2, 2)),
            DMA((2, 2, 2)),
            DMA((2, 2, 2, 2)),
            DMA((2, 2, 2, 2)),
            DMA((2, 2, 2)),
            DMA((2, 2, 2)),
            DMA((16,)),
            DMA((16,)),
        ],
        compiler_params=pltpu.CompilerParams(collective_id=0, has_side_effects=True, vmem_limit_bytes=VMEM_CAP),
        name="gather_blocks",
    )(emb, level)


def pair_kernel(pairs, level, src, tgt, part_out, xbuf, ybuf, turned, top, total, sems):
    k = lax.axis_index("side")

    def fetch(p, slot):
        code = pairs[0, p]
        bs = code // 128
        bt = code % 128
        sz = bs // 16
        sb = bs % 16
        d = bt // 16
        tb = bt % 16
        y0 = d // 2
        x0 = 2 * (d % 2) + (y0 + k) % 2
        f = tb // 6
        line = where(f == 0, y0, x0)
        o = where(f == 0, x0, y0) // 2
        return (
            pltpu.make_async_copy(src.at[sb // 6, sz, sb % 6], xbuf.at[slot], sems.at[0, slot]),
            pltpu.make_async_copy(tgt.at[f, line, o, tb % 6], ybuf.at[slot], sems.at[1, slot]),
        )

    count = pairs[1, 0]

    @pl.when(count > 0)
    def _():
        for copy in fetch(0, 0):
            copy.start()

    for g in range(2):
        rows = level[8 * g : 8 * g + 8].reshape(128, 256)
        turned[g] = rows.T
    top[...] = jnp.full(top.shape, EMPTY, jnp.float32)
    total[...] = jnp.zeros(total.shape, jnp.float32)
    lane = lax.broadcasted_iota(jnp.int32, (256, 128), 1)
    contract = (((1,), (1,)), ((), ()))

    def reduce_to(a, b, g_from, index_from, g_to, index_to):
        bias = jnp.sum(jnp.where(lane == index_from, turned[g_from], 0.0), axis=1, keepdims=True)
        score = lax.dot_general(a, b, contract, preferred_element_type=jnp.float32) * SCALE + bias
        peak = jnp.max(score, axis=0, keepdims=True)
        mass = jnp.sum(jnp.exp2(score - peak), axis=0, keepdims=True)
        old_peak = top[g_to, pl.ds(index_to, 1), :]
        old_mass = total[g_to, pl.ds(index_to, 1), :]
        new_peak = jnp.maximum(old_peak, peak)
        top[g_to, pl.ds(index_to, 1), :] = new_peak
        total[g_to, pl.ds(index_to, 1), :] = old_mass * jnp.exp2(old_peak - new_peak) + mass * jnp.exp2(peak - new_peak)

    def body(p, carry):
        slot = p % 2

        @pl.when(p + 1 < count)
        def _():
            for copy in fetch(p + 1, 1 - slot):
                copy.start()

        for copy in fetch(p, slot):
            copy.wait()
        code = pairs[0, p]
        bs = code // 128
        bt = code % 128
        xs = xbuf[slot]
        ys = ybuf[slot]
        reduce_to(xs, ys, 0, bs, 1, bt)
        reduce_to(ys, xs, 1, bt, 0, bs)
        return carry

    lax.fori_loop(0, count, body, 0)
    for g in range(2):
        mass = total[g]
        value = jnp.where(mass > 0.0, top[g] + jnp.log2(jnp.maximum(mass, 1e-37)), EMPTY)
        part_out[8 * g : 8 * g + 8] = value.reshape(8, 16, 256)


def pair_pass(pairs, level, src, tgt):
    any_spec = pl.BlockSpec(memory_space=pl.ANY)
    vmem = pl.BlockSpec(memory_space=pltpu.VMEM)
    return pl.pallas_call(
        pair_kernel,
        out_shape=jax.ShapeDtypeStruct((16, 16, 256), jnp.float32),
        in_specs=[pl.BlockSpec(memory_space=pltpu.SMEM), vmem, any_spec, any_spec],
        out_specs=vmem,
        scratch_shapes=[
            pltpu.VMEM((2, 256, 256), jnp.bfloat16),
            pltpu.VMEM((2, 256, 256), jnp.bfloat16),
            pltpu.VMEM((2, 256, 128), jnp.float32),
            pltpu.VMEM((2, 128, 256), jnp.float32),
            pltpu.VMEM((2, 128, 256), jnp.float32),
            pltpu.SemaphoreType.DMA((2, 2)),
        ],
        compiler_params=pltpu.CompilerParams(vmem_limit_bytes=VMEM_CAP),
        name="pair_sums",
    )(pairs, level, src, tgt)


def exchange_kernel(last, part, pot, weight, norm, *rest):
    if last:
        pot_out, gathered, send1, recv1 = rest
    else:
        pot_out, level_out, gathered, level, table, send1, recv1, send2, recv2 = rest
    pc = Place()
    barrier = pltpu.get_barrier_semaphore()
    for j in range(16):
        device, me = pc.meeter(j)

        @pl.when(jnp.logical_not(me))
        def _():
            signal(barrier, device)

    pl.semaphore_wait(barrier, pc.peers())

    for j in range(16):
        device, mine = pc.owner(j)
        slot = pc.meet_slot(j)

        @pl.when(jnp.logical_not(mine))
        def _():
            remote(part.at[j], gathered.at[slot], send1.at[j], recv1.at[slot], device).start()

        @pl.when(mine)
        def _():
            gathered[slot] = part[j]

    for j in range(16):
        device, me = pc.meeter(j)

        @pl.when(jnp.logical_not(me))
        def _():
            remote(part.at[j], gathered.at[j], send1.at[j], recv1.at[j], device).wait_recv()

    peak = gathered[0]
    for j in range(1, 16):
        peak = jnp.maximum(peak, gathered[j])
    mass = jnp.zeros_like(peak)
    for j in range(16):
        mass = mass + jnp.exp2(gathered[j] - peak)
    transport = norm[...] - LN2 * (peak + jnp.log2(mass))
    new_pot = 0.5 * (pot[...] + transport)
    pot_out[...] = new_pot
    if not last:
        level[...] = LOG2E * (new_pot + weight[...] - norm[...])
        spread_start(pc, level, table, send2, recv2)
        spread_wait(pc, level, table, send2, recv2)
        level_out[...] = table[...]
    for j in range(16):
        device, mine = pc.owner(j)

        @pl.when(jnp.logical_not(mine))
        def _():
            remote(part.at[j], gathered.at[j], send1.at[j], recv1.at[j], device).wait_send()


def exchange(part, pot, weight, norm, step, last):
    DMA = pltpu.SemaphoreType.DMA
    vmem = pl.BlockSpec(memory_space=pltpu.VMEM)
    small = jax.ShapeDtypeStruct((16, 256), jnp.float32)
    big = jax.ShapeDtypeStruct((16, 16, 256), jnp.float32)
    if last:
        scratch = [pltpu.VMEM((16, 16, 256), jnp.float32), DMA((16,)), DMA((16,))]
        outs, specs = small, vmem
    else:
        scratch = [
            pltpu.VMEM((16, 16, 256), jnp.float32),
            pltpu.VMEM((16, 256), jnp.float32),
            pltpu.VMEM((16, 16, 256), jnp.float32),
            DMA((16,)),
            DMA((16,)),
            DMA((16,)),
            DMA((16,)),
        ]
        outs, specs = (small, big), (vmem, vmem)
    return pl.pallas_call(
        functools.partial(exchange_kernel, last),
        out_shape=outs,
        in_specs=[vmem] * 4,
        out_specs=specs,
        scratch_shapes=scratch,
        compiler_params=pltpu.CompilerParams(
            collective_id=1 + step, has_side_effects=True, vmem_limit_bytes=VMEM_CAP
        ),
        name="exchange_levels",
    )(part, pot, weight, norm)


def per_device(embeds, log_weights, listing):
    emb = embeds[0]
    pairs = listing[0]
    sq = jnp.sum(jnp.square(emb.astype(jnp.float32)), axis=2)
    norm = jnp.pad(INV_BLUR * sq, ((0, 4), (0, 0)))
    weight = jnp.pad(log_weights[0], ((0, 4), (0, 0)))
    own_local = pairs[:, 0] % 12
    far_dev = pairs[:, 1] // 12
    far_local = pairs[:, 1] % 12
    x0 = far_dev // 32
    y0 = (far_dev // 8) % 4
    z0 = far_dev % 8
    code = (z0 * 2 + (x0 + y0) % 2) * 2048 + own_local * 128 + (y0 * 2 + x0 // 2) * 16 + far_local
    code = jnp.pad(code.astype(jnp.float32), (0, 256 - code.shape[0]), constant_values=-1.0)
    level = LOG2E * (weight - norm)
    level = jnp.where(jnp.arange(16)[:, None] == 12, code[None, :], level)
    src, tgt, table, todo = gather(emb, level)
    pot = jnp.zeros_like(norm)
    for step in range(ITERS):
        part = pair_pass(todo, table, src, tgt)
        if step < ITERS - 1:
            pot, table = exchange(part, pot, weight, norm, step, False)
        else:
            pot = exchange(part, pot, weight, norm, step, True)
    return pot[None, :12]


def solution(mesh):
    placed = (
        P("side", ("group", "dev"), None, None),
        P("side", ("group", "dev"), None),
        P("side", ("group", "dev"), None),
    )
    return jax.shard_map(
        per_device,
        mesh=mesh,
        in_specs=placed,
        out_specs=P("side", ("group", "dev"), None),
        check_vma=False,
    )
```

time: 623 us -> 225 us (0.36)
  waiting for transfers between devices: 388 us -> 0 us
  Pallas kernels: 0 us -> 217 us
  matrix products: 92.9 us -> 0 us
  starting transfers between devices: 43 us -> 0 us
  local copies, waits for them, and re-layouts: 45.5 us -> 2.74 us
  blocking collectives: 24.1 us -> 0 us
  other arithmetic: 25.5 us -> 2.77 us
    all_to_all x4 -> x0, waiting for transfers between devices: 386 us -> none  [the longest x1 363 us: per_device(): lax.all_to_all(outgoing, ('group', 'dev'), split_axis=0, concat_axis=0, t...]
    pallas_call x0 -> x7, Pallas kernels: none -> 217 us  [the longest x1 84.1 us: gather(): pl.pallas_call(gather_kernel, out_shape=(jax.ShapeDtypeStruct((2, 8, 6, 2...]
    dot_general x45 -> x0, matrix products: 92.9 us -> none  [the longest x36 72.7 us: block_pass(): jnp.einsum('id,mjd->imj', block_rows, far_rows, preferred_element_type=jn...]
    all_to_all x4 -> x0, starting transfers between devices: 32.6 us -> none  [the longest x3 18.7 us: per_device(): lax.all_to_all(send_level, ('group', 'dev'), split_axis=0, concat_axis=0,...]
    unnamed x11 -> x3, local copies, waits for them, and re-layouts: 27.8 us -> 2.12 us
    all_to_all x1 -> x0, blocking collectives: 24.1 us -> none  [per_device(): lax.all_to_all(wanted, ('group', 'dev'), split_axis=0, concat_axis=0, til...]
    reduce_sum x42 -> x1, other arithmetic: 21.6 us -> 1.89 us  [per_device(): sq = jnp.sum(jnp.square(emb.astype(jnp.float32)), axis=2)]
    while x1 -> x0, local copies, waits for them, and re-layouts: 11.9 us -> none  [per_device(): lax.map(block_pass, (own_blocks, own_sq, cell_far, cell_far_sq, cell_leve...]
  transfers between devices with their start and end apart: 8 -> 0, of which waited for: 5 -> 0; matrix products, arithmetic and copies ran while one was open for 3% -> 0% of each run, Pallas kernels for 0% -> 0%
where the time goes in v1:
time: 225 us; the launch traced here: 223 us
  Pallas kernels  217 us (96%)
  other arithmetic  2.77 us (1%)
  local copies, waits for them, and re-layouts  2.74 us (1%)
    pallas_call x1, Pallas kernels, gather(): pl.pallas_call(gather_kernel, out_shape=(jax.ShapeDtypeStruct((2, 8, 6, 2...  84.1 us
    pallas_call x3, Pallas kernels, exchange(): pl.pallas_call(functools.partial(exchange_kernel, last), out_shape=outs,...  71.6 us
    pallas_call x3, Pallas kernels, pair_pass(): pl.pallas_call(pair_kernel, out_shape=jax.ShapeDtypeStruct((16, 16, 256),...  61.4 us

profile of v1, /device:TPU:1, one launch (start us, length us, event | category | flops | bytes accessed | tf_op | source)
XLA Modules:
  0.0 222.7 jit_solution(17950586984798622291)
XLA Ops:
  0.0 0.8 fusion.9
  0.8 0.7 copy.7
  1.5 1.9 multiply_reduce_fusion
  3.4 0.1 fusion.10
  3.5 0.0 copy-start
  3.5 1.4 copy-done
  4.9 84.1 %gather_blocks.1 = (bf16[2,8,6,256,256]{4,3,2,1,0:T(8,128)(2,1)}, bf16[2,4,2,6,256,256]{5,4,3,2,1,0:T(8,128)(2,1)}, f32[16,16,256]{2,1,0:T(8,128)S(1)}, s32[8,128]{1,0:T(8,128)S(1)}) custom-call(bf16[12,256,256]{2,1,0:T(8,128)(2,1)S(1)} %bitcast.35, f32[16,256]{1,0:T(8,128)S(1)} %get-tuple-element.22.level), custom_call_target="tpu_custom_call" | custom-call | tf_op jit(solution)/shard_map/gather_blocks/pallas_call | solution.py:395
  89.1 20.5 %pair_sums.3.part = f32[16,16,256]{2,1,0:T(8,128)S(1)} custom-call(s32[8,128]{1,0:T(8,128)S(1)} %get-tuple-element.13.pairs, f32[16,16,256]{2,1,0:T(8,128)S(1)} %get-tuple-element.14.level, bf16[2,8,6,256,256]{4,3,2,1,0:T(8,128)(2,1)} %get-tuple-element.15.src, bf16[2,4,2,6,256,256]{5,4,3,2,1,0:T(8,128)(2,1)} %get-tuple-element.16.tgt), custom_call_target="tpu_custom_call" | custom-call | tf_op jit(solution)/shard_map/pair_sums/pallas_call | solution.py:503
  109.5 21.3 %exchange_levels.3 = (f32[16,256]{1,0:T(8,128)S(1)}, f32[16,16,256]{2,1,0:T(8,128)S(1)}) custom-call(f32[16,16,256]{2,1,0:T(8,128)S(1)} %pair_sums.3.part, f32[16,256]{1,0:T(8,128)S(1)} %broadcast_in_dim.26.pot, f32[16,256]{1,0:T(8,128)S(1)} %get-tuple-element.23.weight, f32[16,256]{1,0:T(8,128)S(1)} %get-tuple-element.21.norm), custom_call_target="tpu_custom_call" | custom-call | tf_op jit(solution)/shard_map/exchange_levels/pallas_call | solution.py:597
  130.8 20.5 %pair_sums.4.part = f32[16,16,256]{2,1,0:T(8,128)S(1)} custom-call(s32[8,128]{1,0:T(8,128)S(1)} %get-tuple-element.13.pairs, f32[16,16,256]{2,1,0:T(8,128)S(1)} %get-tuple-element.17.level, bf16[2,8,6,256,256]{4,3,2,1,0:T(8,128)(2,1)} %get-tuple-element.15.src, bf16[2,4,2,6,256,256]{5,4,3,2,1,0:T(8,128)(2,1)} %get-tuple-element.16.tgt), custom_call_target="tpu_custom_call" | custom-call | tf_op jit(solution)/shard_map/pair_sums/pallas_call | solution.py:503
  151.3 27.0 %exchange_levels.4 = (f32[16,256]{1,0:T(8,128)S(1)}, f32[16,16,256]{2,1,0:T(8,128)S(1)}) custom-call(f32[16,16,256]{2,1,0:T(8,128)S(1)} %pair_sums.4.part, f32[16,256]{1,0:T(8,128)S(1)} %get-tuple-element.18.pot, f32[16,256]{1,0:T(8,128)S(1)} %get-tuple-element.23.weight, f32[16,256]{1,0:T(8,128)S(1)} %get-tuple-element.21.norm), custom_call_target="tpu_custom_call" | custom-call | tf_op jit(solution)/shard_map/exchange_levels/pallas_call | solution.py:597
  178.2 20.5 %pair_sums.5.part = f32[16,16,256]{2,1,0:T(8,128)S(1)} custom-call(s32[8,128]{1,0:T(8,128)S(1)} %get-tuple-element.13.pairs, f32[16,16,256]{2,1,0:T(8,128)S(1)} %get-tuple-element.19.level, bf16[2,8,6,256,256]{4,3,2,1,0:T(8,128)(2,1)} %get-tuple-element.15.src, bf16[2,4,2,6,256,256]{5,4,3,2,1,0:T(8,128)(2,1)} %get-tuple-element.16.tgt), custom_call_target="tpu_custom_call" | custom-call | tf_op jit(solution)/shard_map/pair_sums/pallas_call | solution.py:503
  198.7 23.3 %exchange_levels.5 = f32[16,256]{1,0:T(8,128)S(1)} custom-call(f32[16,16,256]{2,1,0:T(8,128)S(1)} %pair_sums.5.part, f32[16,256]{1,0:T(8,128)S(1)} %get-tuple-element.20.pot, f32[16,256]{1,0:T(8,128)S(1)} %get-tuple-element.23.weight, f32[16,256]{1,0:T(8,128)S(1)} %get-tuple-element.21.norm), custom_call_target="tpu_custom_call" | custom-call | tf_op jit(solution)/shard_map/exchange_levels/pallas_call | solution.py:597
  222.1 0.6 copy.4
  (5 shorter events, 0.0 us)
Async XLA Ops:
  3.5 1.4 copy-start

commit v2 on v1

--- a/solution.py
+++ b/solution.py
@@ -10,6 +10,8 @@
 
 MESH = pl.DeviceIdType.MESH
 ITERS = 3
+WIDE = 4
+DEPTH = 16
 NX, NY, NZ = 4, 4, 8
 LOG2E = math.log2(math.e)
 LN2 = math.log(2.0)
@@ -446,11 +448,18 @@
         )
 
     count = pairs[1, 0]
-
-    @pl.when(count > 0)
-    def _():
-        for copy in fetch(0, 0):
-            copy.start()
+    rounds = (count + WIDE - 1) // WIDE
+
+    def fetch_round(r):
+        for u in range(WIDE):
+            p = r * WIDE + u
+            for copy in fetch(p, p % DEPTH):
+                copy.start()
+
+    for r in range(DEPTH // WIDE - 1):
+        @pl.when(r < rounds)
+        def _():
+            fetch_round(r)
 
     for g in range(2):
         rows = level[8 * g : 8 * g + 8].reshape(128, 256)
@@ -460,37 +469,42 @@
     lane = lax.broadcasted_iota(jnp.int32, (256, 128), 1)
     contract = (((1,), (1,)), ((), ()))
 
-    def reduce_to(a, b, g_from, index_from, g_to, index_to):
+    def sums(a, b, g_from, index_from):
         bias = jnp.sum(jnp.where(lane == index_from, turned[g_from], 0.0), axis=1, keepdims=True)
         score = lax.dot_general(a, b, contract, preferred_element_type=jnp.float32) * SCALE + bias
         peak = jnp.max(score, axis=0, keepdims=True)
-        mass = jnp.sum(jnp.exp2(score - peak), axis=0, keepdims=True)
+        return peak, jnp.sum(jnp.exp2(score - peak), axis=0, keepdims=True)
+
+    def merge(peak, mass, g_to, index_to):
         old_peak = top[g_to, pl.ds(index_to, 1), :]
         old_mass = total[g_to, pl.ds(index_to, 1), :]
         new_peak = jnp.maximum(old_peak, peak)
         top[g_to, pl.ds(index_to, 1), :] = new_peak
         total[g_to, pl.ds(index_to, 1), :] = old_mass * jnp.exp2(old_peak - new_peak) + mass * jnp.exp2(peak - new_peak)
 
-    def body(p, carry):
-        slot = p % 2
-
-        @pl.when(p + 1 < count)
-        def _():
-            for copy in fetch(p + 1, 1 - slot):
-                copy.start()
-
-        for copy in fetch(p, slot):
-            copy.wait()
-        code = pairs[0, p]
-        bs = code // 128
-        bt = code % 128
-        xs = xbuf[slot]
-        ys = ybuf[slot]
-        reduce_to(xs, ys, 0, bs, 1, bt)
-        reduce_to(ys, xs, 1, bt, 0, bs)
+    def body(r, carry):
+        @pl.when(r + DEPTH // WIDE - 1 < rounds)
+        def _():
+            fetch_round(r + DEPTH // WIDE - 1)
+
+        for u in range(WIDE):
+            p = r * WIDE + u
+            for copy in fetch(p, p % DEPTH):
+                copy.wait()
+        found = []
+        for u in range(WIDE):
+            p = r * WIDE + u
+            code = pairs[0, p]
+            xs = xbuf[p % DEPTH]
+            ys = ybuf[p % DEPTH]
+            found.append((p, code, sums(xs, ys, 0, code // 128), sums(ys, xs, 1, code % 128)))
+        for p, code, down, across in found:
+            live = p < count
+            for (peak, mass), g_to, index_to in ((down, 1, code % 128), (across, 0, code // 128)):
+                merge(where(live, peak, EMPTY), where(live, mass, 0.0), g_to, index_to)
         return carry
 
-    lax.fori_loop(0, count, body, 0)
+    lax.fori_loop(0, rounds, body, 0)
     for g in range(2):
         mass = total[g]
         value = jnp.where(mass > 0.0, top[g] + jnp.log2(jnp.maximum(mass, 1e-37)), EMPTY)
@@ -506,12 +520,12 @@
         in_specs=[pl.BlockSpec(memory_space=pltpu.SMEM), vmem, any_spec, any_spec],
         out_specs=vmem,
         scratch_shapes=[
-            pltpu.VMEM((2, 256, 256), jnp.bfloat16),
-            pltpu.VMEM((2, 256, 256), jnp.bfloat16),
+            pltpu.VMEM((DEPTH, 256, 256), jnp.bfloat16),
+            pltpu.VMEM((DEPTH, 256, 256), jnp.bfloat16),
             pltpu.VMEM((2, 256, 128), jnp.float32),
             pltpu.VMEM((2, 128, 256), jnp.float32),
             pltpu.VMEM((2, 128, 256), jnp.float32),
-            pltpu.SemaphoreType.DMA((2, 2)),
+            pltpu.SemaphoreType.DMA((2, DEPTH)),
         ],
         compiler_params=pltpu.CompilerParams(vmem_limit_bytes=VMEM_CAP),
         name="pair_sums",

time: 225 us -> 168 us (0.75)
  Pallas kernels: 217 us -> 162 us
    pallas_call x3, Pallas kernels: 61.4 us -> 31.8 us  [pair_pass(): pl.pallas_call(pair_kernel, out_shape=jax.ShapeDtypeStruct((16, 16, 256),...]
    pallas_call x3, Pallas kernels: 71.6 us -> 45.8 us  [exchange(): pl.pallas_call(functools.partial(exchange_kernel, last), out_shape=outs,...]
where the time goes in v2:
time: 168 us; the launch traced here: 167 us
  Pallas kernels  162 us (96%)
  other arithmetic  2.77 us (2%)
  local copies, waits for them, and re-layouts  2.74 us (2%)
    pallas_call x1, Pallas kernels, gather(): pl.pallas_call(gather_kernel, out_shape=(jax.ShapeDtypeStruct((2, 8, 6, 2...  84.1 us
    pallas_call x3, Pallas kernels, exchange(): pl.pallas_call(functools.partial(exchange_kernel, last), out_shape=outs,...  45.8 us
    pallas_call x3, Pallas kernels, pair_pass(): pl.pallas_call(pair_kernel, out_shape=jax.ShapeDtypeStruct((16, 16, 256),...  31.8 us

profile of v2, /device:TPU:1, one launch (start us, length us, event | category | flops | bytes accessed | tf_op | source)
XLA Modules:
  0.0 167.4 jit_solution(166619214200346360)
XLA Ops:
  0.0 0.8 fusion.9
  0.8 0.7 copy.7
  1.5 1.9 %multiply_reduce_fusion = f32[12,256]{1,0:T(8,128)S(1)} fusion(bf16[1,12,256,256]{3,2,1,0:T(8,128)(2,1)} %param.3), kind=kLoop, calls=%fused_computation | loop fusion | flops 2356224 | bytes 1585152 | tf_op jit(solution)/shard_map/reduce_sum | solution.py:627
  3.4 0.1 fusion.10
  3.5 0.0 copy-start
  3.5 1.4 copy-done
  4.9 84.1 %gather_blocks.1 = (bf16[2,8,6,256,256]{4,3,2,1,0:T(8,128)(2,1)}, bf16[2,4,2,6,256,256]{5,4,3,2,1,0:T(8,128)(2,1)}, f32[16,16,256]{2,1,0:T(8,128)S(1)}, s32[8,128]{1,0:T(8,128)S(1)}) custom-call(bf16[12,256,256]{2,1,0:T(8,128)(2,1)S(1)} %bitcast.35, f32[16,256]{1,0:T(8,128)S(1)} %get-tuple-element.22.level), custom_call_target="tpu_custom_call" | custom-call | tf_op jit(solution)/shard_map/gather_blocks/pallas_call | solution.py:397
  89.1 10.6 %pair_sums.3.part = f32[16,16,256]{2,1,0:T(8,128)S(1)} custom-call(s32[8,128]{1,0:T(8,128)S(1)} %get-tuple-element.13.pairs, f32[16,16,256]{2,1,0:T(8,128)S(1)} %get-tuple-element.14.level, bf16[2,8,6,256,256]{4,3,2,1,0:T(8,128)(2,1)} %get-tuple-element.15.src, bf16[2,4,2,6,256,256]{5,4,3,2,1,0:T(8,128)(2,1)} %get-tuple-element.16.tgt), custom_call_target="tpu_custom_call" | custom-call | tf_op jit(solution)/shard_map/pair_sums/pallas_call | solution.py:517
  99.7 14.7 %exchange_levels.3 = (f32[16,256]{1,0:T(8,128)S(1)}, f32[16,16,256]{2,1,0:T(8,128)S(1)}) custom-call(f32[16,16,256]{2,1,0:T(8,128)S(1)} %pair_sums.3.part, f32[16,256]{1,0:T(8,128)S(1)} %broadcast_in_dim.26.pot, f32[16,256]{1,0:T(8,128)S(1)} %get-tuple-element.23.weight, f32[16,256]{1,0:T(8,128)S(1)} %get-tuple-element.21.norm), custom_call_target="tpu_custom_call" | custom-call | tf_op jit(solution)/shard_map/exchange_levels/pallas_call | solution.py:611
  114.4 10.6 %pair_sums.4.part = f32[16,16,256]{2,1,0:T(8,128)S(1)} custom-call(s32[8,128]{1,0:T(8,128)S(1)} %get-tuple-element.13.pairs, f32[16,16,256]{2,1,0:T(8,128)S(1)} %get-tuple-element.17.level, bf16[2,8,6,256,256]{4,3,2,1,0:T(8,128)(2,1)} %get-tuple-element.15.src, bf16[2,4,2,6,256,256]{5,4,3,2,1,0:T(8,128)(2,1)} %get-tuple-element.16.tgt), custom_call_target="tpu_custom_call" | custom-call | tf_op jit(solution)/shard_map/pair_sums/pallas_call | solution.py:517
  125.0 17.6 %exchange_levels.4 = (f32[16,256]{1,0:T(8,128)S(1)}, f32[16,16,256]{2,1,0:T(8,128)S(1)}) custom-call(f32[16,16,256]{2,1,0:T(8,128)S(1)} %pair_sums.4.part, f32[16,256]{1,0:T(8,128)S(1)} %get-tuple-element.18.pot, f32[16,256]{1,0:T(8,128)S(1)} %get-tuple-element.23.weight, f32[16,256]{1,0:T(8,128)S(1)} %get-tuple-element.21.norm), custom_call_target="tpu_custom_call" | custom-call | tf_op jit(solution)/shard_map/exchange_levels/pallas_call | solution.py:611
  142.6 10.6 %pair_sums.5.part = f32[16,16,256]{2,1,0:T(8,128)S(1)} custom-call(s32[8,128]{1,0:T(8,128)S(1)} %get-tuple-element.13.pairs, f32[16,16,256]{2,1,0:T(8,128)S(1)} %get-tuple-element.19.level, bf16[2,8,6,256,256]{4,3,2,1,0:T(8,128)(2,1)} %get-tuple-element.15.src, bf16[2,4,2,6,256,256]{5,4,3,2,1,0:T(8,128)(2,1)} %get-tuple-element.16.tgt), custom_call_target="tpu_custom_call" | custom-call | tf_op jit(solution)/shard_map/pair_sums/pallas_call | solution.py:517
  153.2 13.5 %exchange_levels.5 = f32[16,256]{1,0:T(8,128)S(1)} custom-call(f32[16,16,256]{2,1,0:T(8,128)S(1)} %pair_sums.5.part, f32[16,256]{1,0:T(8,128)S(1)} %get-tuple-element.20.pot, f32[16,256]{1,0:T(8,128)S(1)} %get-tuple-element.23.weight, f32[16,256]{1,0:T(8,128)S(1)} %get-tuple-element.21.norm), custom_call_target="tpu_custom_call" | custom-call | tf_op jit(solution)/shard_map/exchange_levels/pallas_call | solution.py:611
  166.8 0.6 copy.4
  (5 shorter events, 0.0 us)
Async XLA Ops:
  3.5 1.4 copy-start

commit v3 on v1

v3 whole, which is shorter than its diff:
```python
import math

import jax
import jax.numpy as jnp
from jax import lax
from jax.experimental import pallas as pl
from jax.experimental.pallas import tpu as pltpu
from jax.sharding import PartitionSpec as P

MESH = pl.DeviceIdType.MESH
ITERS = 3
NX, NY, NZ = 4, 4, 8
LOG2E = math.log2(math.e)
LN2 = math.log(2.0)
INV_BLUR = 10.0
SCALE = 2.0 * INV_BLUR * LOG2E
EMPTY = -1e30
VMEM_CAP = 50 * 1024 * 1024


def where(pred, a, b):
    return jnp.where(pred, a, b)


class Place:
    def __init__(self):
        self.k = lax.axis_index("side")
        self.x = lax.axis_index("group")
        dev = lax.axis_index("dev")
        self.y = dev // NZ
        self.z = dev % NZ
        self.kq = (self.x + self.y) % 2
        self.own_slot = self.y * 2 + self.x // 2

    def dev(self, k, x, y, z):
        return (k, x, y * NZ + z)

    def owner(self, j):
        if j < 8:
            return self.dev(jnp.int32(0), self.x, self.y, jnp.int32(j)), jnp.logical_and(self.k == 0, self.z == j)
        d = j - 8
        y0 = d // 2
        x0 = 2 * (d % 2) + (y0 + self.k) % 2
        me = jnp.logical_and(self.k == 1, jnp.logical_and(self.x == x0, self.y == y0))
        return self.dev(jnp.int32(1), x0, jnp.int32(y0), self.z), me

    def meeter(self, j):
        src = self.k == 0
        kk = where(src, j % 2, self.kq)
        xx = where(src, self.x, j % 4)
        yy = where(src, self.y, j // 4)
        zz = where(src, j // 2, self.z)
        me = jnp.logical_and(
            jnp.logical_and(kk == self.k, xx == self.x), jnp.logical_and(yy == self.y, zz == self.z)
        )
        return self.dev(kk, xx, yy, zz), me

    def peers(self):
        return 16 - where(jnp.logical_or(self.k == 0, self.kq == 1), 1, 0)

    def level_slot(self):
        return where(self.k == 0, self.z, 8 + self.own_slot)

    def meet_slot(self, j):
        return self.z * 2 + self.k if j < 8 else self.y * 4 + self.x


def remote(src, dst, send_sem, recv_sem, device):
    return pltpu.make_async_remote_copy(
        src_ref=src, dst_ref=dst, send_sem=send_sem, recv_sem=recv_sem, device_id=device, device_id_type=MESH
    )


def spread_start(pc, level, table, send_sem, recv_sem):
    slot = pc.level_slot()
    for j in range(16):
        device, me = pc.meeter(j)

        @pl.when(jnp.logical_not(me))
        def _():
            remote(level, table.at[slot], send_sem.at[j], recv_sem.at[slot], device).start()

        @pl.when(me)
        def _():
            table[slot] = level[...]


def spread_wait(pc, level, table, send_sem, recv_sem):
    for j in range(16):
        device, me = pc.meeter(j)
        owner, mine = pc.owner(j)

        @pl.when(jnp.logical_not(mine))
        def _():
            remote(level, table.at[j], send_sem.at[j], recv_sem.at[j], owner).wait_recv()

    for j in range(16):
        device, me = pc.meeter(j)

        @pl.when(jnp.logical_not(me))
        def _():
            remote(level, table.at[j], send_sem.at[j], recv_sem.at[j], device).wait_send()


def signal(sem, device):
    pl.semaphore_signal(sem, inc=1, device_id=device, device_id_type=MESH)


def sinkhorn_kernel(
    emb, meet, weight, norm, pot_out,
    src, tgt, table, level, plan, todo, turned, parts, gathered, pot, found,
    todo_sem, local_sem, own_sem, z_send, z_recv, sib_send, sib_recv,
    first_send, first_recv, next_send, next_recv, relay_send, relay_recv,
    plan_send, plan_recv, lv_send, lv_recv, part_send, part_recv,
):
    pc = Place()
    k, x, y, z = pc.k, pc.x, pc.y, pc.z
    sibling = pc.dev(1 - k, x, y, z)
    zdev = [pc.dev(k, x, y, (z + 1) % NZ), pc.dev(k, x, y, (z + NZ - 1) % NZ)]
    xdev = [pc.dev(k, (x + 1) % NX, y, z), pc.dev(k, (x + NX - 1) % NX, y, z)]
    ydev = [pc.dev(k, x, (y + 1) % NY, z), pc.dev(k, x, (y + NY - 1) % NY, z)]

    barrier = pltpu.get_barrier_semaphore()
    for device in [sibling] + zdev + xdev + ydev:
        signal(barrier, device)
    for j in range(16):
        device, mine = pc.owner(j)

        @pl.when(jnp.logical_not(mine))
        def _():
            signal(barrier, device)

    pl.semaphore_wait(barrier, 7 + pc.peers())

    native = k == pc.kq

    def src_at(h, z0, s):
        return src.at[z0, pl.ds(6 * h + 3 * s, 3)]

    def tgt_at(f, line, o, s, core=k):
        if f == 0:
            return tgt.at[line * 2 + o, pl.ds(3 * s, 3)]
        return tgt.at[(2 * o + (line + core) % 2) * 2 + line // 2, pl.ds(6 + 3 * s, 3)]

    line_of = [y, x]
    spot_of = [x, y]
    spread_dev = [xdev, ydev]
    onward_dev = [ydev, xdev]

    @pl.when(k == 0)
    def _():
        for h in (1, 0):
            for s in range(2):
                part = emb.at[pl.ds(6 * h + 3 * s, 3)]
                remote(part, src_at(h, z, s), own_sem.at[0, h, s], own_sem.at[1, h, s], sibling).start()
        for h in range(2):
            for s in range(2):
                part = emb.at[pl.ds(6 * h + 3 * s, 3)]
                pltpu.make_async_copy(part, src_at(h, z, s), local_sem.at[h, s]).start()

    @pl.when(jnp.logical_and(k == 1, pc.kq == 1))
    def _():
        for f in range(2):
            for s in range(2):
                part = emb.at[pl.ds(6 * f + 3 * s, 3)]
                pltpu.make_async_copy(part, tgt_at(f, line_of[f], spot_of[f] // 2, s), local_sem.at[f, s]).start()

    @pl.when(jnp.logical_and(k == 1, pc.kq == 0))
    def _():
        for f in range(2):
            for s in range(2):
                part = emb.at[pl.ds(6 * f + 3 * s, 3)]
                remote(
                    part, tgt_at(f, line_of[f], spot_of[f] // 2, s, pc.kq), own_sem.at[0, f, s], own_sem.at[1, f, s], sibling
                ).start()

    level[...] = LOG2E * (weight[...] - norm[...])
    spread_start(pc, level, table.at[0], lv_send.at[0], lv_recv.at[0])

    def plan_copy(j, slot, device):
        return remote(meet.at[j], plan.at[slot], plan_send.at[j], plan_recv.at[slot], device)

    @pl.when(k == 0)
    def _():
        for j in range(16):
            device, me = pc.meeter(j)

            @pl.when(jnp.logical_not(me))
            def _():
                plan_copy(j, z, device).start()

            @pl.when(me)
            def _():
                plan[z] = meet[j]

    def z_copy(way, r, s):
        z0 = (z - r + NZ) % NZ if way == 0 else (z + r) % NZ
        part = src.at[z0, pl.ds(6 * k + 3 * s, 3)]
        return remote(part, part, z_send.at[way, r, s], z_recv.at[way, r, s], zdev[way])

    def z_landed(way, r, s):
        z0 = (z - r - 1 + NZ) % NZ if way == 0 else (z + r + 1) % NZ
        part = src.at[z0, pl.ds(6 * k + 3 * s, 3)]
        return remote(part, part, z_send.at[way, r, s], z_recv.at[way, r, s], zdev[way])

    def sib_copy(way, r, s):
        z0 = (z - r - 1 + NZ) % NZ if way == 0 else (z + r + 1) % NZ
        part = src.at[z0, pl.ds(6 * k + 3 * s, 3)]
        return remote(part, part, sib_send.at[way, r, s], sib_recv.at[way, r, s], sibling)

    def sib_landed(way, r, s):
        z0 = (z - r - 1 + NZ) % NZ if way == 0 else (z + r + 1) % NZ
        part = src.at[z0, pl.ds(6 * (1 - k) + 3 * s, 3)]
        return remote(part, part, sib_send.at[way, r, s], sib_recv.at[way, r, s], sibling)

    def z_subs(way, r):
        return (0, 1) if r < 3 else (way,)

    for s in range(2):
        @pl.when(k == 0)
        def _():
            part = emb.at[pl.ds(3 * s, 3)]
            pltpu.make_async_copy(part, src_at(0, z, s), local_sem.at[0, s]).wait()

        @pl.when(k == 1)
        def _():
            part = src_at(1, z, s)
            remote(part, part, own_sem.at[0, 1, s], own_sem.at[1, 1, s], sibling).wait_recv()

        for way in range(2):
            z_copy(way, 0, s).start()

    def first_copy(f, way, o, s):
        part = tgt_at(f, line_of[f], o, s)
        return remote(part, part, first_send.at[f, way, s], first_recv.at[f, way, s], spread_dev[f][way])

    def next_copy(f, way, o, s):
        part = tgt_at(f, line_of[f], o, s)
        return remote(part, part, next_send.at[f, way, o, s], next_recv.at[f, way, o, s], onward_dev[f][way])

    def from_line(f, way):
        n = line_of[f]
        return (n + 3) % 4 if way == 0 else (n + 1) % 4

    def next_landed(f, way, o, s):
        part = tgt_at(f, from_line(f, way), o, s)
        return remote(part, part, next_send.at[f, way, o, s], next_recv.at[f, way, o, s], onward_dev[f][way])

    def relay_copy(f, way, o):
        part = tgt_at(f, from_line(f, way), o, way)
        return remote(part, part, relay_send.at[f, way, o], relay_recv.at[f, way, o], onward_dev[f][way])

    def relay_landed(f, way, o):
        part = tgt_at(f, (line_of[f] + 2) % 4, o, way)
        return remote(part, part, relay_send.at[f, way, o], relay_recv.at[f, way, o], onward_dev[f][way])

    home = [spot_of[f] // 2 for f in range(2)]
    near = [[((spot_of[f] + 3) % 4) // 2, ((spot_of[f] + 1) % 4) // 2] for f in range(2)]

    @pl.when(native)
    def _():
        for s in range(2):
            for f in range(2):
                part = tgt_at(f, line_of[f], home[f], s)

                @pl.when(k == 1)
                def _():
                    pltpu.make_async_copy(emb.at[pl.ds(6 * f + 3 * s, 3)], part, local_sem.at[f, s]).wait()

                @pl.when(k == 0)
                def _():
                    remote(part, part, own_sem.at[0, f, s], own_sem.at[1, f, s], sibling).wait_recv()

                for way in range(2):
                    first_copy(f, way, home[f], s).start()
        for s in range(2):
            for f in range(2):
                for way in range(2):
                    next_copy(f, way, home[f], s).start()

    def z_forward(r):
        for s in range(2):
            for way in range(2):
                if s in z_subs(way, r):
                    z_landed(way, r, s).wait_recv()
                    if r < 3 and s in z_subs(way, r + 1):
                        z_copy(way, r + 1, s).start()
                    sib_copy(way, r, s).start()

    z_forward(0)

    @pl.when(jnp.logical_not(native))
    def _():
        for s in range(2):
            for f in range(2):
                for way in range(2):
                    o = near[f][way]
                    first_copy(f, way, o, s).wait_recv()
                    if s == way:
                        first_copy(f, way, o, s).start()
                    for w in range(2):
                        next_copy(f, w, o, s).start()

    z_forward(1)

    @pl.when(native)
    def _():
        for f in range(2):
            for way in range(2):
                o = 1 - home[f]
                first_copy(f, way, o, way).wait_recv()
                for w in range(2):
                    next_copy(f, w, o, way).start()

    def onward(nth):
        for s in range(2):
            for f in range(2):
                o = home[f] if nth == 0 else 1 - home[f]
                for way in range(2):
                    next_landed(f, way, o, s).wait_recv()
                    if s == way:
                        relay_copy(f, way, o).start()

    onward(0)
    z_forward(2)
    onward(1)
    z_forward(3)

    for f in range(2):
        for way in range(2):
            for o in range(2):
                relay_landed(f, way, o).wait_recv()
    for r in range(4):
        for way in range(2):
            for s in z_subs(way, r):
                sib_landed(way, r, s).wait_recv()

    @pl.when(k == 1)
    def _():
        for s in range(2):
            part = src_at(0, z, s)
            remote(part, part, own_sem.at[0, 0, s], own_sem.at[1, 0, s], sibling).wait_recv()

    @pl.when(k == 0)
    def _():
        for s in range(2):
            part = emb.at[pl.ds(6 + 3 * s, 3)]
            pltpu.make_async_copy(part, src_at(1, z, s), local_sem.at[1, s]).wait()
        for h in range(2):
            for s in range(2):
                part = emb.at[pl.ds(6 * h + 3 * s, 3)]
                remote(part, src_at(h, z, s), own_sem.at[0, h, s], own_sem.at[1, h, s], sibling).wait_send()

    @pl.when(jnp.logical_and(k == 1, pc.kq == 0))
    def _():
        for f in range(2):
            for s in range(2):
                part = emb.at[pl.ds(6 * f + 3 * s, 3)]
                remote(
                    part, tgt_at(f, line_of[f], home[f], s, pc.kq), own_sem.at[0, f, s], own_sem.at[1, f, s], sibling
                ).wait_send()

    for r in range(4):
        for way in range(2):
            for s in z_subs(way, r):
                z_copy(way, r, s).wait_send()
                sib_copy(way, r, s).wait_send()
    for f in range(2):
        for way in range(2):
            for s in range(2):
                @pl.when(native)
                def _():
                    first_copy(f, way, home[f], s).wait_send()

            @pl.when(jnp.logical_not(native))
            def _():
                first_copy(f, way, near[f][way], way).wait_send()

            for o in range(2):
                relay_copy(f, way, o).wait_send()
                for s in range(2):
                    next_copy(f, way, o, s).wait_send()


    for j in range(8):
        device, mine = pc.owner(j)

        @pl.when(jnp.logical_not(mine))
        def _():
            plan_copy(0, j, device).wait_recv()

    listed = pltpu.make_async_copy(plan, todo, todo_sem)
    listed.start()
    listed.wait()

    @pl.when(k == 0)
    def _():
        for j in range(16):
            device, me = pc.meeter(j)

            @pl.when(jnp.logical_not(me))
            def _():
                plan_copy(j, z, device).wait_send()

    lane = lax.broadcasted_iota(jnp.int32, (256, 128), 1)
    contract = (((1,), (1,)), ((), ()))
    pot[...] = jnp.zeros(pot.shape, jnp.float32)
    found[...] = jnp.zeros(found.shape, jnp.float32)

    def log_sums(a, b, g_from, index_from):
        bias = jnp.sum(jnp.where(lane == index_from, turned[g_from], 0.0), axis=1, keepdims=True)
        score = lax.dot_general(a, b, contract, preferred_element_type=jnp.float32) * SCALE + bias
        peak = jnp.max(score, axis=0, keepdims=True)
        return peak + jnp.log2(jnp.sum(jnp.exp2(score - peak), axis=0, keepdims=True))

    for step in range(ITERS):
        turn = step % 2
        spread_wait(pc, level, table.at[turn], lv_send.at[turn], lv_recv.at[turn])
        for g in range(2):
            turned[g] = table[turn, 8 * g : 8 * g + 8].reshape(128, 256).T

        def line_of_pairs(a, carry):
            sums = []
            for d in range(8):
                code = jnp.maximum(todo[a, d, 0] - 1, 0)
                bs = code // 16
                bt = code % 16
                xs = src[a, bs]
                ys = tgt[d, bt]
                sums.append((log_sums(xs, ys, 0, a * 16 + bs), log_sums(ys, xs, 1, d * 16 + bt)))
            for d in range(8):
                down, across = sums[d]
                parts[8 + d, pl.ds(a, 1), :] = down
                parts[a, pl.ds(d, 1), :] = across
            return carry

        lax.fori_loop(0, 8, line_of_pairs, 0)

        def part_copy(j, slot, device):
            return remote(
                parts.at[j], gathered.at[turn, slot], part_send.at[turn, j], part_recv.at[turn, slot], device
            )

        for j in range(16):
            device, mine = pc.owner(j)
            slot = pc.meet_slot(j)

            @pl.when(jnp.logical_not(mine))
            def _():
                part_copy(j, slot, device).start()

            @pl.when(mine)
            def _():
                gathered[turn, slot] = parts[j]

        for j in range(16):
            device, me = pc.meeter(j)

            @pl.when(jnp.logical_not(me))
            def _():
                part_copy(j, j, device).wait_recv()

        block_of = (meet[...] + 15) // 16 - 1
        for half in range(2):
            cols = pl.ds(128 * half, 128)
            rows = gathered[turn, :, :, cols]
            for b in range(12):
                held = jnp.where(block_of == b, rows, EMPTY)
                peak = jnp.max(jnp.max(held, axis=0), axis=0, keepdims=True)
                mass = jnp.sum(jnp.sum(jnp.exp2(held - peak), axis=0), axis=0, keepdims=True)
                found[b : b + 1, cols] = peak + jnp.log2(mass)
        new_pot = 0.5 * (pot[...] + norm[...] - LN2 * found[...])
        pot[...] = new_pot
        if step < ITERS - 1:
            level[...] = LOG2E * (new_pot + weight[...] - norm[...])
            spread_start(pc, level, table.at[1 - turn], lv_send.at[1 - turn], lv_recv.at[1 - turn])
        for j in range(16):
            device, mine = pc.owner(j)

            @pl.when(jnp.logical_not(mine))
            def _():
                part_copy(j, j, device).wait_send()

    pot_out[...] = pot[0:12]


def per_device(embeds, log_weights, listing):
    emb = embeds[0]
    pairs = listing[0]
    sq = jnp.sum(jnp.square(emb.astype(jnp.float32)), axis=2)
    norm = jnp.pad(INV_BLUR * sq, ((0, 4), (0, 0)))
    weight = jnp.pad(log_weights[0], ((0, 4), (0, 0)))
    own_local = pairs[:, 0] % 12
    far_dev = pairs[:, 1] // 12
    far_local = pairs[:, 1] % 12
    fx = far_dev // 32
    fy = (far_dev // 8) % 4
    fz = far_dev % 8
    place_src = (fz * 2 + (fx + fy) % 2) * 8 + fy * 2 + fx // 2
    place_tgt = (fy * 4 + fx) * 8 + fz
    place = jnp.where(lax.axis_index("side") == 0, place_src, place_tgt)
    hot = place[:, None] == jnp.arange(128)[None, :]
    meet = jnp.sum(jnp.where(hot, (own_local * 16 + far_local + 1)[:, None], 0), axis=0)
    meet = jnp.broadcast_to(meet.reshape(16, 8, 1), (16, 8, 128))
    DMA = pltpu.SemaphoreType.DMA
    any_spec = pl.BlockSpec(memory_space=pl.ANY)
    vmem = pl.BlockSpec(memory_space=pltpu.VMEM)
    f32 = jnp.float32
    pot = pl.pallas_call(
        sinkhorn_kernel,
        out_shape=jax.ShapeDtypeStruct((12, 256), f32),
        in_specs=[any_spec, vmem, vmem, vmem],
        out_specs=vmem,
        scratch_shapes=[
            pltpu.VMEM((8, 12, 256, 256), jnp.bfloat16),
            pltpu.VMEM((8, 12, 256, 256), jnp.bfloat16),
            pltpu.VMEM((2, 16, 16, 256), f32),
            pltpu.VMEM((16, 256), f32),
            pltpu.VMEM((8, 8, 128), jnp.int32),
            pltpu.SMEM((8, 8, 128), jnp.int32),
            pltpu.VMEM((2, 256, 128), f32),
            pltpu.VMEM((16, 8, 256), f32),
            pltpu.VMEM((2, 16, 8, 256), f32),
            pltpu.VMEM((16, 256), f32),
            pltpu.VMEM((16, 256), f32),
            DMA,
            DMA((2, 2)),
            DMA((2, 2, 2)),
            DMA((2, 4, 2)),
            DMA((2, 4, 2)),
            DMA((2, 4, 2)),
            DMA((2, 4, 2)),
            DMA((2, 2, 2)),
            DMA((2, 2, 2)),
            DMA((2, 2, 2, 2)),
            DMA((2, 2, 2, 2)),
            DMA((2, 2, 2)),
            DMA((2, 2, 2)),
            DMA((16,)),
            DMA((8,)),
            DMA((2, 16)),
            DMA((2, 16)),
            DMA((2, 16)),
            DMA((2, 16)),
        ],
        compiler_params=pltpu.CompilerParams(collective_id=0, has_side_effects=True, vmem_limit_bytes=VMEM_CAP),
        name="sinkhorn",
    )(emb, meet, weight, norm)
    return pot[None]


def solution(mesh):
    placed = (
        P("side", ("group", "dev"), None, None),
        P("side", ("group", "dev"), None),
        P("side", ("group", "dev"), None),
    )
    return jax.shard_map(
        per_device,
        mesh=mesh,
        in_specs=placed,
        out_specs=P("side", ("group", "dev"), None),
        check_vma=False,
    )
```

time: 225 us -> 157 us (0.70)
  Pallas kernels: 217 us -> 152 us
    pallas_call x7 -> x1, Pallas kernels: 217 us -> 152 us  [per_device(): pl.pallas_call(sinkhorn_kernel, out_shape=jax.ShapeDtypeStruct((12, 256),...]
where the time goes in v3:
time: 157 us
  Pallas kernels  152 us (97%)
  other arithmetic  2.85 us (2%)
    pallas_call x1, Pallas kernels, per_device(): pl.pallas_call(sinkhorn_kernel, out_shape=jax.ShapeDtypeStruct((12, 256),...  152 us

profile of v3, /device:TPU:1, one launch (start us, length us, event | category | flops | bytes accessed | tf_op | source)
XLA Modules:
  0.0 156.8 jit_solution(435472620880260365)
XLA Ops:
  0.0 0.0 copy-start
  0.0 0.9 fusion.2
  0.9 0.1 select_reduce_fusion
  1.0 0.1 broadcast_in_dim.30
  1.0 0.7 copy.9
  1.8 1.9 %multiply_reduce_fusion = f32[12,256]{1,0:T(8,128)S(1)} fusion(bf16[1,12,256,256]{3,2,1,0:T(8,128)(2,1)} %param.3), kind=kLoop, calls=%fused_computation | loop fusion | flops 2356224 | bytes 1585152 | tf_op jit(solution)/shard_map/reduce_sum | solution.py:490
  3.7 0.1 broadcast_in_dim.31.meet
  3.8 0.0 copy-done
  3.8 152.4 %sinkhorn.1 = f32[12,256]{1,0:T(8,128)S(1)} custom-call(bf16[12,256,256]{2,1,0:T(8,128)(2,1)S(1)} %bitcast.11, s32[16,8,128]{2,1,0:T(8,128)S(1)} %broadcast_in_dim.31.meet, f32[16,256]{1,0:T(8,128)S(1)} %pad.7.weight, f32[16,256]{1,0:T(8,128)S(1)} %pad.8.norm), custom_call_target="tpu_custom_call" | custom-call | tf_op jit(solution)/shard_map/sinkhorn/pallas_call | solution.py:509
  156.2 0.6 copy.6
  (3 shorter events, 0.0 us)
Async XLA Ops:
  0.0 3.8 %copy-start = (bf16[1,12,256,256]{3,2,1,0:T(8,128)(2,1)S(1)}, bf16[1,12,256,256]{3,2,1,0:T(8,128)(2,1)}, u32[]{:S(2)}) copy-start(bf16[1,12,256,256]{3,2,1,0:T(8,128)(2,1)} %param.3) | copy-start | bytes 4718596

commit v4 on v3

--- a/solution.py
+++ b/solution.py
@@ -9,6 +9,7 @@
 
 MESH = pl.DeviceIdType.MESH
 ITERS = 3
+MIDDLE = 3
 NX, NY, NZ = 4, 4, 8
 LOG2E = math.log2(math.e)
 LN2 = math.log(2.0)
@@ -35,14 +36,17 @@
     def dev(self, k, x, y, z):
         return (k, x, y * NZ + z)
 
-    def owner(self, j):
-        if j < 8:
-            return self.dev(jnp.int32(0), self.x, self.y, jnp.int32(j)), jnp.logical_and(self.k == 0, self.z == j)
-        d = j - 8
+    def source_owner(self, a):
+        return self.dev(jnp.int32(0), self.x, self.y, a), jnp.logical_and(self.k == 0, self.z == a)
+
+    def target_owner(self, d):
         y0 = d // 2
         x0 = 2 * (d % 2) + (y0 + self.k) % 2
         me = jnp.logical_and(self.k == 1, jnp.logical_and(self.x == x0, self.y == y0))
-        return self.dev(jnp.int32(1), x0, jnp.int32(y0), self.z), me
+        return self.dev(jnp.int32(1), x0, y0, self.z), me
+
+    def owner(self, j):
+        return self.source_owner(jnp.int32(j)) if j < 8 else self.target_owner(jnp.int32(j - 8))
 
     def meeter(self, j):
         src = self.k == 0
@@ -61,8 +65,8 @@
     def level_slot(self):
         return where(self.k == 0, self.z, 8 + self.own_slot)
 
-    def meet_slot(self, j):
-        return self.z * 2 + self.k if j < 8 else self.y * 4 + self.x
+    def meet_slot(self, side):
+        return self.z * 2 + self.k if side == 0 else self.y * 4 + self.x
 
 
 def remote(src, dst, send_sem, recv_sem, device):
@@ -85,17 +89,18 @@
             table[slot] = level[...]
 
 
-def spread_wait(pc, level, table, send_sem, recv_sem):
+def spread_landed(pc, level, table, send_sem, recv_sem, side):
+    for j in range(8 * side, 8 * side + 8):
+        owner, mine = pc.owner(j)
+
+        @pl.when(jnp.logical_not(mine))
+        def _():
+            remote(level, table.at[j], send_sem.at[j], recv_sem.at[j], owner).wait_recv()
+
+
+def spread_sent(pc, level, table, send_sem, recv_sem):
     for j in range(16):
         device, me = pc.meeter(j)
-        owner, mine = pc.owner(j)
-
-        @pl.when(jnp.logical_not(mine))
-        def _():
-            remote(level, table.at[j], send_sem.at[j], recv_sem.at[j], owner).wait_recv()
-
-    for j in range(16):
-        device, me = pc.meeter(j)
 
         @pl.when(jnp.logical_not(me))
         def _():
@@ -107,9 +112,9 @@
 
 
 def sinkhorn_kernel(
-    emb, meet, weight, norm, pot_out,
-    src, tgt, table, level, plan, todo, turned, parts, gathered, pot, found,
-    todo_sem, local_sem, own_sem, z_send, z_recv, sib_send, sib_recv,
+    emb, meet, weight, pot_out,
+    src, tgt, mine_blocks, norm, table, level, plan, todo, turned, parts, gathered, pot, found,
+    todo_sem, norm_sem, local_sem, own_sem, z_out, first_out, next_out, z_send, z_recv, sib_send, sib_recv,
     first_send, first_recv, next_send, next_recv, relay_send, relay_recv,
     plan_send, plan_recv, lv_send, lv_recv, part_send, part_recv,
 ):
@@ -147,34 +152,92 @@
     spread_dev = [xdev, ydev]
     onward_dev = [ydev, xdev]
 
+    own_line = pc.own_slot
+
+    def z_first(way, h, s):
+        part = emb.at[pl.ds(6 * h + 3 * s, 3)]
+        z1 = (z + 1) % NZ if way == 0 else (z + NZ - 1) % NZ
+        return remote(
+            part, src_at(h, z, s), z_out.at[way, h, s], z_recv.at[way, 0, s], pc.dev(jnp.int32(h), x, y, z1)
+        )
+
+    def to_core(device):
+        return (pc.kq,) + device[1:]
+
+    def tgt_first(f, way, s):
+        part = emb.at[pl.ds(6 * f + 3 * s, 3)]
+        home_at = tgt.at[own_line, pl.ds(6 * f + 3 * s, 3)]
+        return remote(part, home_at, first_out.at[f, way, s], first_recv.at[f, way, s], to_core(spread_dev[f][way]))
+
+    def tgt_next(f, way, s):
+        part = emb.at[pl.ds(6 * f + 3 * s, 3)]
+        home_at = tgt.at[own_line, pl.ds(6 * f + 3 * s, 3)]
+        return remote(
+            part, home_at, next_out.at[f, way, s], next_recv.at[f, way, spot_of[f] // 2, s], to_core(onward_dev[f][way])
+        )
+
+    def norm_copy():
+        return pltpu.make_async_copy(emb, mine_blocks, norm_sem)
+
+    def src_local():
+        return pltpu.make_async_copy(emb, src.at[z], local_sem)
+
+    def src_sibling():
+        return remote(emb, src.at[z], own_sem.at[0], own_sem.at[1], sibling)
+
+    def tgt_local():
+        return pltpu.make_async_copy(emb, tgt.at[own_line], local_sem)
+
+    def tgt_sibling():
+        return remote(emb, tgt.at[own_line], own_sem.at[0], own_sem.at[1], sibling)
+
     @pl.when(k == 0)
     def _():
-        for h in (1, 0):
-            for s in range(2):
-                part = emb.at[pl.ds(6 * h + 3 * s, 3)]
-                remote(part, src_at(h, z, s), own_sem.at[0, h, s], own_sem.at[1, h, s], sibling).start()
-        for h in range(2):
-            for s in range(2):
-                part = emb.at[pl.ds(6 * h + 3 * s, 3)]
-                pltpu.make_async_copy(part, src_at(h, z, s), local_sem.at[h, s]).start()
-
-    @pl.when(jnp.logical_and(k == 1, pc.kq == 1))
-    def _():
-        for f in range(2):
-            for s in range(2):
-                part = emb.at[pl.ds(6 * f + 3 * s, 3)]
-                pltpu.make_async_copy(part, tgt_at(f, line_of[f], spot_of[f] // 2, s), local_sem.at[f, s]).start()
-
-    @pl.when(jnp.logical_and(k == 1, pc.kq == 0))
-    def _():
-        for f in range(2):
-            for s in range(2):
-                part = emb.at[pl.ds(6 * f + 3 * s, 3)]
-                remote(
-                    part, tgt_at(f, line_of[f], spot_of[f] // 2, s, pc.kq), own_sem.at[0, f, s], own_sem.at[1, f, s], sibling
-                ).start()
-
-    level[...] = LOG2E * (weight[...] - norm[...])
+        for s in range(2):
+            for way in range(2):
+                for h in range(2):
+                    z_first(way, h, s).start()
+        src_local().start()
+        src_sibling().start()
+
+    @pl.when(k == 1)
+    def _():
+        for s in range(2):
+            for f in range(2):
+                for way in range(2):
+                    tgt_first(f, way, s).start()
+        for s in range(2):
+            for f in range(2):
+                for way in range(2):
+                    tgt_next(f, way, s).start()
+
+        @pl.when(pc.kq == 1)
+        def _():
+            tgt_local().start()
+
+        @pl.when(pc.kq == 0)
+        def _():
+            tgt_sibling().start()
+
+    norm_copy().start()
+    norm_copy().wait()
+    ones = jnp.ones((8, 256), jnp.bfloat16)
+    norm[...] = jnp.zeros(norm.shape, jnp.float32)
+    level[...] = jnp.zeros(level.shape, jnp.float32)
+
+    def norm_of(b, carry):
+        value = mine_blocks[b].astype(jnp.float32)
+        square = value * value
+        high = square.astype(jnp.bfloat16)
+        low = (square - high.astype(jnp.float32)).astype(jnp.bfloat16)
+        across = (((1,), (1,)), ((), ()))
+        total = lax.dot_general(ones, high, across, preferred_element_type=jnp.float32)
+        total = total + lax.dot_general(ones, low, across, preferred_element_type=jnp.float32)
+        norm[pl.ds(b, 1), :] = INV_BLUR * total[0:1]
+        return carry
+
+    lax.fori_loop(0, 12, norm_of, 0)
+    level[0:12] = LOG2E * (weight[...] - norm[0:12])
     spread_start(pc, level, table.at[0], lv_send.at[0], lv_recv.at[0])
 
     def plan_copy(j, slot, device):
@@ -216,20 +279,6 @@
     def z_subs(way, r):
         return (0, 1) if r < 3 else (way,)
 
-    for s in range(2):
-        @pl.when(k == 0)
-        def _():
-            part = emb.at[pl.ds(3 * s, 3)]
-            pltpu.make_async_copy(part, src_at(0, z, s), local_sem.at[0, s]).wait()
-
-        @pl.when(k == 1)
-        def _():
-            part = src_at(1, z, s)
-            remote(part, part, own_sem.at[0, 1, s], own_sem.at[1, 1, s], sibling).wait_recv()
-
-        for way in range(2):
-            z_copy(way, 0, s).start()
-
     def first_copy(f, way, o, s):
         part = tgt_at(f, line_of[f], o, s)
         return remote(part, part, first_send.at[f, way, s], first_recv.at[f, way, s], spread_dev[f][way])
@@ -256,27 +305,6 @@
 
     home = [spot_of[f] // 2 for f in range(2)]
     near = [[((spot_of[f] + 3) % 4) // 2, ((spot_of[f] + 1) % 4) // 2] for f in range(2)]
-
-    @pl.when(native)
-    def _():
-        for s in range(2):
-            for f in range(2):
-                part = tgt_at(f, line_of[f], home[f], s)
-
-                @pl.when(k == 1)
-                def _():
-                    pltpu.make_async_copy(emb.at[pl.ds(6 * f + 3 * s, 3)], part, local_sem.at[f, s]).wait()
-
-                @pl.when(k == 0)
-                def _():
-                    remote(part, part, own_sem.at[0, f, s], own_sem.at[1, f, s], sibling).wait_recv()
-
-                for way in range(2):
-                    first_copy(f, way, home[f], s).start()
-        for s in range(2):
-            for f in range(2):
-                for way in range(2):
-                    next_copy(f, way, home[f], s).start()
 
     def z_forward(r):
         for s in range(2):
@@ -335,52 +363,59 @@
             for s in z_subs(way, r):
                 sib_landed(way, r, s).wait_recv()
 
+    @pl.when(k == 0)
+    def _():
+        src_local().wait()
+        src_sibling().wait_send()
+        for s in range(2):
+            for way in range(2):
+                for h in range(2):
+                    z_first(way, h, s).wait_send()
+
+        @pl.when(pc.kq == 0)
+        def _():
+            tgt_sibling().wait_recv()
+
     @pl.when(k == 1)
     def _():
-        for s in range(2):
-            part = src_at(0, z, s)
-            remote(part, part, own_sem.at[0, 0, s], own_sem.at[1, 0, s], sibling).wait_recv()
-
-    @pl.when(k == 0)
-    def _():
-        for s in range(2):
-            part = emb.at[pl.ds(6 + 3 * s, 3)]
-            pltpu.make_async_copy(part, src_at(1, z, s), local_sem.at[1, s]).wait()
-        for h in range(2):
-            for s in range(2):
-                part = emb.at[pl.ds(6 * h + 3 * s, 3)]
-                remote(part, src_at(h, z, s), own_sem.at[0, h, s], own_sem.at[1, h, s], sibling).wait_send()
-
-    @pl.when(jnp.logical_and(k == 1, pc.kq == 0))
-    def _():
-        for f in range(2):
-            for s in range(2):
-                part = emb.at[pl.ds(6 * f + 3 * s, 3)]
-                remote(
-                    part, tgt_at(f, line_of[f], home[f], s, pc.kq), own_sem.at[0, f, s], own_sem.at[1, f, s], sibling
-                ).wait_send()
+        src_sibling().wait_recv()
+
+        @pl.when(pc.kq == 1)
+        def _():
+            tgt_local().wait()
+
+        @pl.when(pc.kq == 0)
+        def _():
+            tgt_sibling().wait_send()
+
+        for s in range(2):
+            for f in range(2):
+                for way in range(2):
+                    tgt_first(f, way, s).wait_send()
+                    tgt_next(f, way, s).wait_send()
 
     for r in range(4):
         for way in range(2):
             for s in z_subs(way, r):
-                z_copy(way, r, s).wait_send()
+                if r > 0:
+                    z_copy(way, r, s).wait_send()
                 sib_copy(way, r, s).wait_send()
     for f in range(2):
         for way in range(2):
-            for s in range(2):
-                @pl.when(native)
-                def _():
-                    first_copy(f, way, home[f], s).wait_send()
-
-            @pl.when(jnp.logical_not(native))
-            def _():
-                first_copy(f, way, near[f][way], way).wait_send()
-
             for o in range(2):
                 relay_copy(f, way, o).wait_send()
-                for s in range(2):
-                    next_copy(f, way, o, s).wait_send()
-
+
+            @pl.when(native)
+            def _():
+                next_copy(f, way, 1 - home[f], 0).wait_send()
+                next_copy(f, way, 1 - home[f], 1).wait_send()
+
+            @pl.when(jnp.logical_not(native))
+            def _():
+                first_copy(f, way, near[f][way], way).wait_send()
+                for o in range(2):
+                    for s in range(2):
+                        next_copy(f, way, o, s).wait_send()
 
     for j in range(8):
         device, mine = pc.owner(j)
@@ -413,52 +448,67 @@
         peak = jnp.max(score, axis=0, keepdims=True)
         return peak + jnp.log2(jnp.sum(jnp.exp2(score - peak), axis=0, keepdims=True))
 
-    for step in range(ITERS):
+    def level_copies(turn):
+        return (pc, level, table.at[turn], lv_send.at[turn], lv_recv.at[turn])
+
+    def take_levels(side, step):
+        spread_landed(*level_copies(step % 2), side)
+        turned[side] = table[step % 2, 8 * side : 8 * side + 8].reshape(128, 256).T
+
+    def part_copy(side, step, i, slot, device):
         turn = step % 2
-        spread_wait(pc, level, table.at[turn], lv_send.at[turn], lv_recv.at[turn])
-        for g in range(2):
-            turned[g] = table[turn, 8 * g : 8 * g + 8].reshape(128, 256).T
-
-        def line_of_pairs(a, carry):
+        return remote(
+            parts.at[8 * side + i], gathered.at[turn, slot], part_send.at[turn, 8 * side + i], part_recv.at[turn, slot],
+            device,
+        )
+
+    def sums_of(side, step):
+        def body(i, carry):
             sums = []
-            for d in range(8):
+            for u in range(8):
+                a, d = (i, u) if side == 0 else (u, i)
                 code = jnp.maximum(todo[a, d, 0] - 1, 0)
                 bs = code // 16
                 bt = code % 16
                 xs = src[a, bs]
                 ys = tgt[d, bt]
-                sums.append((log_sums(xs, ys, 0, a * 16 + bs), log_sums(ys, xs, 1, d * 16 + bt)))
-            for d in range(8):
-                down, across = sums[d]
-                parts[8 + d, pl.ds(a, 1), :] = down
-                parts[a, pl.ds(d, 1), :] = across
+                if side == 0:
+                    sums.append(log_sums(ys, xs, 1, d * 16 + bt))
+                else:
+                    sums.append(log_sums(xs, ys, 0, a * 16 + bs))
+            for u in range(8):
+                parts[8 * side + i, u : u + 1, :] = sums[u]
+            device, mine = pc.source_owner(i) if side == 0 else pc.target_owner(i)
+            slot = pc.meet_slot(side)
+
+            @pl.when(jnp.logical_not(mine))
+            def _():
+                part_copy(side, step, i, slot, device).start()
+
+            @pl.when(mine)
+            def _():
+                gathered[step % 2, slot] = parts[8 * side + i]
+
             return carry
 
-        lax.fori_loop(0, 8, line_of_pairs, 0)
-
-        def part_copy(j, slot, device):
-            return remote(
-                parts.at[j], gathered.at[turn, slot], part_send.at[turn, j], part_recv.at[turn, slot], device
-            )
-
-        for j in range(16):
-            device, mine = pc.owner(j)
-            slot = pc.meet_slot(j)
+        return body
+
+    def parts_sent(side, step):
+        for j in range(8):
+            device, mine = pc.owner(8 * side + j)
 
             @pl.when(jnp.logical_not(mine))
             def _():
-                part_copy(j, slot, device).start()
-
-            @pl.when(mine)
-            def _():
-                gathered[turn, slot] = parts[j]
-
+                part_copy(side, step, j, 0, device).wait_send()
+
+    def combine(step):
+        turn = step % 2
         for j in range(16):
             device, me = pc.meeter(j)
 
             @pl.when(jnp.logical_not(me))
             def _():
-                part_copy(j, j, device).wait_recv()
+                part_copy(0, step, 0, j, device).wait_recv()
 
         block_of = (meet[...] + 15) // 16 - 1
         for half in range(2):
@@ -472,24 +522,44 @@
         new_pot = 0.5 * (pot[...] + norm[...] - LN2 * found[...])
         pot[...] = new_pot
         if step < ITERS - 1:
-            level[...] = LOG2E * (new_pot + weight[...] - norm[...])
-            spread_start(pc, level, table.at[1 - turn], lv_send.at[1 - turn], lv_recv.at[1 - turn])
-        for j in range(16):
-            device, mine = pc.owner(j)
-
-            @pl.when(jnp.logical_not(mine))
-            def _():
-                part_copy(j, j, device).wait_send()
-
+            spread_sent(*level_copies(turn))
+            level[0:12] = LOG2E * (new_pot[0:12] + weight[...] - norm[0:12])
+            spread_start(*level_copies(1 - turn))
+
+    order = []
+    for step in range(ITERS):
+        order += [(0, step), (1, step)] if step % 2 == 0 else [(1, step), (0, step)]
+    for n, (side, step) in enumerate(order):
+        take_levels(1 - side, step)
+        if step > 0:
+            parts_sent(side, step - 1)
+        body = sums_of(side, step)
+        if n == 0:
+            lax.fori_loop(0, 8, body, 0)
+        else:
+            lax.fori_loop(0, MIDDLE, body, 0)
+            last_side, last_step = order[n - 1]
+
+            @pl.when(k == last_side)
+            def _():
+                combine(last_step)
+
+            lax.fori_loop(MIDDLE, 8, body, 0)
+    last_side, last_step = order[-1]
+
+    @pl.when(k == last_side)
+    def _():
+        combine(last_step)
+
+    for side in range(2):
+        parts_sent(side, ITERS - 1)
+    spread_sent(*level_copies((ITERS - 1) % 2))
     pot_out[...] = pot[0:12]
 
 
 def per_device(embeds, log_weights, listing):
     emb = embeds[0]
     pairs = listing[0]
-    sq = jnp.sum(jnp.square(emb.astype(jnp.float32)), axis=2)
-    norm = jnp.pad(INV_BLUR * sq, ((0, 4), (0, 0)))
-    weight = jnp.pad(log_weights[0], ((0, 4), (0, 0)))
     own_local = pairs[:, 0] % 12
     far_dev = pairs[:, 1] // 12
     far_local = pairs[:, 1] % 12
@@ -509,11 +579,13 @@
     pot = pl.pallas_call(
         sinkhorn_kernel,
         out_shape=jax.ShapeDtypeStruct((12, 256), f32),
-        in_specs=[any_spec, vmem, vmem, vmem],
+        in_specs=[any_spec, vmem, vmem],
         out_specs=vmem,
         scratch_shapes=[
             pltpu.VMEM((8, 12, 256, 256), jnp.bfloat16),
             pltpu.VMEM((8, 12, 256, 256), jnp.bfloat16),
+            pltpu.VMEM((12, 256, 256), jnp.bfloat16),
+            pltpu.VMEM((16, 256), f32),
             pltpu.VMEM((2, 16, 16, 256), f32),
             pltpu.VMEM((16, 256), f32),
             pltpu.VMEM((8, 8, 128), jnp.int32),
@@ -524,7 +596,11 @@
             pltpu.VMEM((16, 256), f32),
             pltpu.VMEM((16, 256), f32),
             DMA,
-            DMA((2, 2)),
+            DMA,
+            DMA,
+            DMA((2,)),
+            DMA((2, 2, 2)),
+            DMA((2, 2, 2)),
             DMA((2, 2, 2)),
             DMA((2, 4, 2)),
             DMA((2, 4, 2)),
@@ -545,7 +621,7 @@
         ],
         compiler_params=pltpu.CompilerParams(collective_id=0, has_side_effects=True, vmem_limit_bytes=VMEM_CAP),
         name="sinkhorn",
-    )(emb, meet, weight, norm)
+    )(emb, meet, log_weights[0])
     return pot[None]
 
 

time: 157 us -> 140 us (0.89)
  Pallas kernels: 152 us -> 135 us
  other arithmetic: 2.85 us -> 0.89 us
    pallas_call x1, Pallas kernels: 152 us -> 135 us  [per_device(): pl.pallas_call(sinkhorn_kernel, out_shape=jax.ShapeDtypeStruct((12, 256),...]
    reduce_sum x1 -> x0, other arithmetic: 1.89 us -> none  [per_device(): sq = jnp.sum(jnp.square(emb.astype(jnp.float32)), axis=2)]
where the time goes in v4:
time: 140 us; the launch traced here: 138 us
  Pallas kernels  135 us (96%)
  local copies, waits for them, and re-layouts  2.91 us (2%)
    pallas_call x1, Pallas kernels, per_device(): pl.pallas_call(sinkhorn_kernel, out_shape=jax.ShapeDtypeStruct((12, 256),...  135 us

profile of v4, /device:TPU:1, one launch (start us, length us, event | category | flops | bytes accessed | tf_op | source)
XLA Modules:
  0.0 138.3 jit_solution(5179345078923410105)
XLA Ops:
  0.0 0.8 fusion.2
  0.8 0.1 select_reduce_fusion
  0.9 0.1 broadcast_in_dim.30
  1.0 0.7 copy.9
  1.7 0.1 broadcast_in_dim.31.meet
  1.8 0.0 copy-start
  1.8 1.4 %copy-done = bf16[1,12,256,256]{3,2,1,0:T(8,128)(2,1)S(1)} copy-done((bf16[1,12,256,256]{3,2,1,0:T(8,128)(2,1)S(1)}, bf16[1,12,256,256]{3,2,1,0:T(8,128)(2,1)}, u32[]{:S(2)}) %copy-start) | copy-done | bytes 1572888
  3.2 134.5 %sinkhorn.1 = f32[12,256]{1,0:T(8,128)S(1)} custom-call(bf16[12,256,256]{2,1,0:T(8,128)(2,1)S(1)} %bitcast.10, s32[16,8,128]{2,1,0:T(8,128)S(1)} %broadcast_in_dim.31.meet, f32[12,256]{1,0:T(8,128)S(1)} %bitcast.11), custom_call_target="tpu_custom_call" | custom-call | tf_op jit(solution)/shard_map/sinkhorn/pallas_call | solution.py:579
  137.7 0.6 copy.6
Async XLA Ops:
  1.8 1.4 %copy-start = (bf16[1,12,256,256]{3,2,1,0:T(8,128)(2,1)S(1)}, bf16[1,12,256,256]{3,2,1,0:T(8,128)(2,1)}, u32[]{:S(2)}) copy-start(bf16[1,12,256,256]{3,2,1,0:T(8,128)(2,1)} %param.3) | copy-start | bytes 4718596

commit v5 on v4

--- a/solution.py
+++ b/solution.py
@@ -9,7 +9,7 @@
 
 MESH = pl.DeviceIdType.MESH
 ITERS = 3
-MIDDLE = 3
+LATE = 3
 NX, NY, NZ = 4, 4, 8
 LOG2E = math.log2(math.e)
 LN2 = math.log(2.0)
@@ -112,9 +112,9 @@
 
 
 def sinkhorn_kernel(
-    emb, meet, weight, pot_out,
-    src, tgt, mine_blocks, norm, table, level, plan, todo, turned, parts, gathered, pot, found,
-    todo_sem, norm_sem, local_sem, own_sem, z_out, first_out, next_out, z_send, z_recv, sib_send, sib_recv,
+    emb, pairs, weights, pot_out,
+    src, tgt, meet, weight, mine_blocks, norm, table, level, plan, todo, turned, turned_one, parts, gathered, pot, found,
+    todo_sem, norm_sem, weight_sem, local_sem, own_sem, z_out, first_out, next_out, z_send, z_recv, sib_send, sib_recv,
     first_send, first_recv, next_send, next_recv, relay_send, relay_recv,
     plan_send, plan_recv, lv_send, lv_recv, part_send, part_recv,
 ):
@@ -220,6 +220,23 @@
             tgt_sibling().start()
 
     norm_copy().start()
+    weight_copy = pltpu.make_async_copy(weights, weight, weight_sem)
+    weight_copy.start()
+
+    own_local = pairs[:, 0:1] - 12 * (x * 32 + y * 8 + z)
+    far = pairs[:, 1:2]
+    far_dev = (far * 43691) >> 19
+    far_local = far - 12 * far_dev
+    fx = far_dev >> 5
+    fy = (far_dev >> 3) & 3
+    fz = far_dev & 7
+    place_src = (fz * 2 + ((fx + fy) & 1)) * 8 + fy * 2 + (fx >> 1)
+    place_tgt = (fy * 4 + fx) * 8 + fz
+    place = jnp.where(k == 0, place_src, place_tgt)
+    hot = place == lax.broadcasted_iota(jnp.int32, (60, 128), 1)
+    line = jnp.sum(jnp.where(hot, own_local * 16 + far_local + 1, 0), axis=0, keepdims=True)
+    meet[...] = jnp.broadcast_to(line, (128, 128)).T.reshape(16, 8, 128)
+    weight_copy.wait()
     norm_copy().wait()
     ones = jnp.ones((8, 256), jnp.bfloat16)
     norm[...] = jnp.zeros(norm.shape, jnp.float32)
@@ -442,8 +459,9 @@
     pot[...] = jnp.zeros(pot.shape, jnp.float32)
     found[...] = jnp.zeros(found.shape, jnp.float32)
 
-    def log_sums(a, b, g_from, index_from):
-        bias = jnp.sum(jnp.where(lane == index_from, turned[g_from], 0.0), axis=1, keepdims=True)
+    lane16 = lax.broadcasted_iota(jnp.int32, (256, 16), 1)
+
+    def log_sums(a, b, bias):
         score = lax.dot_general(a, b, contract, preferred_element_type=jnp.float32) * SCALE + bias
         peak = jnp.max(score, axis=0, keepdims=True)
         return peak + jnp.log2(jnp.sum(jnp.exp2(score - peak), axis=0, keepdims=True))
@@ -462,36 +480,70 @@
             device,
         )
 
-    def sums_of(side, step):
-        def body(i, carry):
+    def part_out(side, step, i):
+        device, mine = pc.source_owner(i) if side == 0 else pc.target_owner(i)
+        slot = pc.meet_slot(side)
+
+        @pl.when(jnp.logical_not(mine))
+        def _():
+            part_copy(side, step, i, slot, device).start()
+
+        @pl.when(mine)
+        def _():
+            gathered[step % 2, slot] = parts[8 * side + i]
+
+    def sums_of(side, step, outer, staged=False, before=None):
+        def body(pair, carry):
+            if before is not None:
+                before(pair)
+            if staged:
+                for w in range(2):
+                    i = pair * 2 + w
+                    owner, mine = pc.source_owner(i) if outer == 0 else pc.target_owner(i)
+                    _, _, rows, sent, landed = level_copies(step % 2)
+                    j = 8 * outer + i
+
+                    @pl.when(jnp.logical_not(mine))
+                    def _():
+                        remote(level, rows.at[j], sent.at[j], landed.at[j], owner).wait_recv()
+
+                for w in range(2):
+                    turned_one[w] = table[step % 2, 8 * outer + pair * 2 + w].T
             sums = []
-            for u in range(8):
-                a, d = (i, u) if side == 0 else (u, i)
-                code = jnp.maximum(todo[a, d, 0] - 1, 0)
-                bs = code // 16
-                bt = code % 16
-                xs = src[a, bs]
-                ys = tgt[d, bt]
-                if side == 0:
-                    sums.append(log_sums(ys, xs, 1, d * 16 + bt))
-                else:
-                    sums.append(log_sums(xs, ys, 0, a * 16 + bs))
-            for u in range(8):
-                parts[8 * side + i, u : u + 1, :] = sums[u]
-            device, mine = pc.source_owner(i) if side == 0 else pc.target_owner(i)
-            slot = pc.meet_slot(side)
-
-            @pl.when(jnp.logical_not(mine))
-            def _():
-                part_copy(side, step, i, slot, device).start()
-
-            @pl.when(mine)
-            def _():
-                gathered[step % 2, slot] = parts[8 * side + i]
-
+            for w in range(2):
+                i = pair * 2 + w
+                for u in range(8):
+                    a, d = (i, u) if outer == 0 else (u, i)
+                    code = jnp.maximum(todo[a, d, 0] - 1, 0)
+                    bs = code // 16
+                    bt = code % 16
+                    xs = src[a, bs]
+                    ys = tgt[d, bt]
+                    if side == 0:
+                        left, right, row, base = ys, xs, bt, d
+                    else:
+                        left, right, row, base = xs, ys, bs, a
+                    if staged:
+                        bias = jnp.sum(jnp.where(lane16 == row, turned_one[w], 0.0), axis=1, keepdims=True)
+                    else:
+                        bias = jnp.sum(jnp.where(lane == base * 16 + row, turned[1 - side], 0.0), axis=1, keepdims=True)
+                    sums.append(log_sums(left, right, bias))
+            for w in range(2):
+                i = pair * 2 + w
+                for u in range(8):
+                    if outer == side:
+                        parts[8 * side + i, u : u + 1, :] = sums[8 * w + u]
+                    else:
+                        parts[8 * side + u, pl.ds(i, 1), :] = sums[8 * w + u]
+            if outer == side:
+                for w in range(2):
+                    part_out(side, step, pair * 2 + w)
             return carry
 
-        return body
+        lax.fori_loop(0, 4, body, 0)
+        if outer != side:
+            for i in range(8):
+                part_out(side, step, jnp.int32(i))
 
     def parts_sent(side, step):
         for j in range(8):
@@ -526,52 +578,43 @@
             level[0:12] = LOG2E * (new_pot[0:12] + weight[...] - norm[0:12])
             spread_start(*level_copies(1 - turn))
 
-    order = []
-    for step in range(ITERS):
-        order += [(0, step), (1, step)] if step % 2 == 0 else [(1, step), (0, step)]
-    for n, (side, step) in enumerate(order):
-        take_levels(1 - side, step)
-        if step > 0:
-            parts_sent(side, step - 1)
-        body = sums_of(side, step)
-        if n == 0:
-            lax.fori_loop(0, 8, body, 0)
-        else:
-            lax.fori_loop(0, MIDDLE, body, 0)
-            last_side, last_step = order[n - 1]
-
-            @pl.when(k == last_side)
-            def _():
-                combine(last_step)
-
-            lax.fori_loop(MIDDLE, 8, body, 0)
-    last_side, last_step = order[-1]
-
-    @pl.when(k == last_side)
-    def _():
-        combine(last_step)
-
-    for side in range(2):
-        parts_sent(side, ITERS - 1)
-    spread_sent(*level_copies((ITERS - 1) % 2))
+    def combine_at(side, step, turn):
+        def before(i):
+            @pl.when(jnp.logical_and(k == side, i == turn))
+            def _():
+                combine(step)
+
+        return before
+
+    take_levels(1, 0)
+    sums_of(0, 0, 0)
+    take_levels(0, 0)
+    sums_of(1, 0, 1, before=combine_at(0, 0, z // 2))
+    parts_sent(1, 0)
+    sums_of(1, 1, 0, staged=True, before=combine_at(1, 0, pc.own_slot // 2))
+    parts_sent(0, 0)
+    sums_of(0, 1, 1, staged=True, before=combine_at(1, 1, LATE))
+
+    @pl.when(k == 0)
+    def _():
+        combine(1)
+
+    take_levels(1, 2)
+    parts_sent(0, 1)
+    sums_of(0, 2, 0)
+    take_levels(0, 2)
+    parts_sent(1, 1)
+    sums_of(1, 2, 1)
+    combine(2)
+    parts_sent(0, 2)
+    parts_sent(1, 2)
+    spread_sent(*level_copies(0))
     pot_out[...] = pot[0:12]
 
 
 def per_device(embeds, log_weights, listing):
     emb = embeds[0]
     pairs = listing[0]
-    own_local = pairs[:, 0] % 12
-    far_dev = pairs[:, 1] // 12
-    far_local = pairs[:, 1] % 12
-    fx = far_dev // 32
-    fy = (far_dev // 8) % 4
-    fz = far_dev % 8
-    place_src = (fz * 2 + (fx + fy) % 2) * 8 + fy * 2 + fx // 2
-    place_tgt = (fy * 4 + fx) * 8 + fz
-    place = jnp.where(lax.axis_index("side") == 0, place_src, place_tgt)
-    hot = place[:, None] == jnp.arange(128)[None, :]
-    meet = jnp.sum(jnp.where(hot, (own_local * 16 + far_local + 1)[:, None], 0), axis=0)
-    meet = jnp.broadcast_to(meet.reshape(16, 8, 1), (16, 8, 128))
     DMA = pltpu.SemaphoreType.DMA
     any_spec = pl.BlockSpec(memory_space=pl.ANY)
     vmem = pl.BlockSpec(memory_space=pltpu.VMEM)
@@ -579,11 +622,13 @@
     pot = pl.pallas_call(
         sinkhorn_kernel,
         out_shape=jax.ShapeDtypeStruct((12, 256), f32),
-        in_specs=[any_spec, vmem, vmem],
+        in_specs=[any_spec, vmem, any_spec],
         out_specs=vmem,
         scratch_shapes=[
             pltpu.VMEM((8, 12, 256, 256), jnp.bfloat16),
             pltpu.VMEM((8, 12, 256, 256), jnp.bfloat16),
+            pltpu.VMEM((16, 8, 128), jnp.int32),
+            pltpu.VMEM((12, 256), f32),
             pltpu.VMEM((12, 256, 256), jnp.bfloat16),
             pltpu.VMEM((16, 256), f32),
             pltpu.VMEM((2, 16, 16, 256), f32),
@@ -591,10 +636,12 @@
             pltpu.VMEM((8, 8, 128), jnp.int32),
             pltpu.SMEM((8, 8, 128), jnp.int32),
             pltpu.VMEM((2, 256, 128), f32),
+            pltpu.VMEM((2, 256, 16), f32),
             pltpu.VMEM((16, 8, 256), f32),
             pltpu.VMEM((2, 16, 8, 256), f32),
             pltpu.VMEM((16, 256), f32),
             pltpu.VMEM((16, 256), f32),
+            DMA,
             DMA,
             DMA,
             DMA,
@@ -621,7 +668,7 @@
         ],
         compiler_params=pltpu.CompilerParams(collective_id=0, has_side_effects=True, vmem_limit_bytes=VMEM_CAP),
         name="sinkhorn",
-    )(emb, meet, log_weights[0])
+    )(emb, pairs, log_weights[0])
     return pot[None]
 
 

time: 140 us -> 138 us (0.986)
  Pallas kernels: 135 us -> 132 us
    pallas_call x1, Pallas kernels: 135 us -> 132 us  [per_device(): pl.pallas_call(sinkhorn_kernel, out_shape=jax.ShapeDtypeStruct((12, 256),...]
where the time goes in v5:
time: 138 us; the launch traced here: 136 us
  Pallas kernels  132 us (96%)
  local copies, waits for them, and re-layouts  3.51 us (3%)
    pallas_call x1, Pallas kernels, per_device(): pl.pallas_call(sinkhorn_kernel, out_shape=jax.ShapeDtypeStruct((12, 256),...  132 us

profile of v5, /device:TPU:1, one launch (start us, length us, event | category | flops | bytes accessed | tf_op | source)
XLA Modules:
  0.0 136.0 jit_solution(17089061388222539483)
XLA Ops:
  0.0 0.7 copy.8
  0.7 0.8 copy.4.pairs
  1.5 0.0 copy-start
  1.5 1.4 %copy-done = bf16[1,12,256,256]{3,2,1,0:T(8,128)(2,1)S(1)} copy-done((bf16[1,12,256,256]{3,2,1,0:T(8,128)(2,1)S(1)}, bf16[1,12,256,256]{3,2,1,0:T(8,128)(2,1)}, u32[]{:S(2)}) %copy-start) | copy-done | bytes 1572888
  2.9 132.5 %sinkhorn.1 = f32[12,256]{1,0:T(8,128)S(1)} custom-call(bf16[12,256,256]{2,1,0:T(8,128)(2,1)S(1)} %bitcast.6, s32[60,2]{1,0:T(8,128)S(1)} %copy.4.pairs, f32[12,256]{1,0:T(8,128)S(1)} %bitcast.8), custom_call_target="tpu_custom_call" | custom-call | tf_op jit(solution)/shard_map/sinkhorn/pallas_call | solution.py:622
  135.4 0.6 copy.5
Async XLA Ops:
  1.5 1.4 %copy-start = (bf16[1,12,256,256]{3,2,1,0:T(8,128)(2,1)S(1)}, bf16[1,12,256,256]{3,2,1,0:T(8,128)(2,1)}, u32[]{:S(2)}) copy-start(bf16[1,12,256,256]{3,2,1,0:T(8,128)(2,1)} %param.3) | copy-start | bytes 4718596

commit v6 on v5

--- a/solution.py
+++ b/solution.py
@@ -368,6 +368,33 @@
 
     onward(0)
     z_forward(2)
+
+    for j in range(8):
+        device, mine = pc.owner(j)
+
+        @pl.when(jnp.logical_not(mine))
+        def _():
+            plan_copy(0, j, device).wait_recv()
+
+    listed = pltpu.make_async_copy(plan, todo, todo_sem)
+    listed.start()
+    listed.wait()
+
+    @pl.when(k == 0)
+    def _():
+        for j in range(16):
+            device, me = pc.meeter(j)
+
+            @pl.when(jnp.logical_not(me))
+            def _():
+                plan_copy(j, z, device).wait_send()
+
+    for side in range(2):
+        spread_landed(pc, level, table.at[0], lv_send.at[0], lv_recv.at[0], side)
+        turned[side] = table[0, 8 * side : 8 * side + 8].reshape(128, 256).T
+    pot[...] = jnp.zeros(pot.shape, jnp.float32)
+    found[...] = jnp.zeros(found.shape, jnp.float32)
+
     onward(1)
     z_forward(3)
 
@@ -411,53 +438,8 @@
                     tgt_first(f, way, s).wait_send()
                     tgt_next(f, way, s).wait_send()
 
-    for r in range(4):
-        for way in range(2):
-            for s in z_subs(way, r):
-                if r > 0:
-                    z_copy(way, r, s).wait_send()
-                sib_copy(way, r, s).wait_send()
-    for f in range(2):
-        for way in range(2):
-            for o in range(2):
-                relay_copy(f, way, o).wait_send()
-
-            @pl.when(native)
-            def _():
-                next_copy(f, way, 1 - home[f], 0).wait_send()
-                next_copy(f, way, 1 - home[f], 1).wait_send()
-
-            @pl.when(jnp.logical_not(native))
-            def _():
-                first_copy(f, way, near[f][way], way).wait_send()
-                for o in range(2):
-                    for s in range(2):
-                        next_copy(f, way, o, s).wait_send()
-
-    for j in range(8):
-        device, mine = pc.owner(j)
-
-        @pl.when(jnp.logical_not(mine))
-        def _():
-            plan_copy(0, j, device).wait_recv()
-
-    listed = pltpu.make_async_copy(plan, todo, todo_sem)
-    listed.start()
-    listed.wait()
-
-    @pl.when(k == 0)
-    def _():
-        for j in range(16):
-            device, me = pc.meeter(j)
-
-            @pl.when(jnp.logical_not(me))
-            def _():
-                plan_copy(j, z, device).wait_send()
-
     lane = lax.broadcasted_iota(jnp.int32, (256, 128), 1)
     contract = (((1,), (1,)), ((), ()))
-    pot[...] = jnp.zeros(pot.shape, jnp.float32)
-    found[...] = jnp.zeros(found.shape, jnp.float32)
 
     lane16 = lax.broadcasted_iota(jnp.int32, (256, 16), 1)
 
@@ -586,9 +568,7 @@
 
         return before
 
-    take_levels(1, 0)
     sums_of(0, 0, 0)
-    take_levels(0, 0)
     sums_of(1, 0, 1, before=combine_at(0, 0, z // 2))
     parts_sent(1, 0)
     sums_of(1, 1, 0, staged=True, before=combine_at(1, 0, pc.own_slot // 2))
@@ -609,6 +589,29 @@
     parts_sent(0, 2)
     parts_sent(1, 2)
     spread_sent(*level_copies(0))
+    for r in range(4):
+        for way in range(2):
+            for s in z_subs(way, r):
+                if r > 0:
+                    z_copy(way, r, s).wait_send()
+                sib_copy(way, r, s).wait_send()
+    for f in range(2):
+        for way in range(2):
+            for o in range(2):
+                relay_copy(f, way, o).wait_send()
+
+            @pl.when(native)
+            def _():
+                next_copy(f, way, 1 - home[f], 0).wait_send()
+                next_copy(f, way, 1 - home[f], 1).wait_send()
+
+            @pl.when(jnp.logical_not(native))
+            def _():
+                first_copy(f, way, near[f][way], way).wait_send()
+                for o in range(2):
+                    for s in range(2):
+                        next_copy(f, way, o, s).wait_send()
+
     pot_out[...] = pot[0:12]
 
 

time: 138 us -> 136 us (0.986)
    pallas_call x1, Pallas kernels: 132 us -> 131 us  [per_device(): pl.pallas_call(sinkhorn_kernel, out_shape=jax.ShapeDtypeStruct((12, 256),...]
where the time goes in v6:
time: 136 us; the launch traced here: 135 us
  Pallas kernels  131 us (96%)
  local copies, waits for them, and re-layouts  3.51 us (3%)
    pallas_call x1, Pallas kernels, per_device(): pl.pallas_call(sinkhorn_kernel, out_shape=jax.ShapeDtypeStruct((12, 256),...  131 us

profile of v6, /device:TPU:1, one launch (start us, length us, event | category | flops | bytes accessed | tf_op | source)
XLA Modules:
  0.0 134.5 jit_solution(2844477933218082498)
XLA Ops:
  0.0 0.7 copy.8
  0.7 0.8 copy.4.pairs
  1.5 0.0 copy-start
  1.5 1.4 %copy-done = bf16[1,12,256,256]{3,2,1,0:T(8,128)(2,1)S(1)} copy-done((bf16[1,12,256,256]{3,2,1,0:T(8,128)(2,1)S(1)}, bf16[1,12,256,256]{3,2,1,0:T(8,128)(2,1)}, u32[]{:S(2)}) %copy-start) | copy-done | bytes 1572888
  2.9 131.0 %sinkhorn.1 = f32[12,256]{1,0:T(8,128)S(1)} custom-call(bf16[12,256,256]{2,1,0:T(8,128)(2,1)S(1)} %bitcast.6, s32[60,2]{1,0:T(8,128)S(1)} %copy.4.pairs, f32[12,256]{1,0:T(8,128)S(1)} %bitcast.8), custom_call_target="tpu_custom_call" | custom-call | tf_op jit(solution)/shard_map/sinkhorn/pallas_call | solution.py:625
  133.9 0.6 copy.5
Async XLA Ops:
  1.5 1.4 %copy-start = (bf16[1,12,256,256]{3,2,1,0:T(8,128)(2,1)S(1)}, bf16[1,12,256,256]{3,2,1,0:T(8,128)(2,1)}, u32[]{:S(2)}) copy-start(bf16[1,12,256,256]{3,2,1,0:T(8,128)(2,1)} %param.3) | copy-start | bytes 4718596

commit v7 on v6

--- a/solution.py
+++ b/solution.py
@@ -367,7 +367,6 @@
                         relay_copy(f, way, o).start()
 
     onward(0)
-    z_forward(2)
 
     for j in range(8):
         device, mine = pc.owner(j)
@@ -396,6 +395,7 @@
     found[...] = jnp.zeros(found.shape, jnp.float32)
 
     onward(1)
+    z_forward(2)
     z_forward(3)
 
     for f in range(2):

time: 136 us -> 137 us (level)
  no operation moved by 1% of the time
where the time goes in v7:
time: 137 us; the launch traced here: 135 us
  Pallas kernels  132 us (96%)
  local copies, waits for them, and re-layouts  3.51 us (3%)
    pallas_call x1, Pallas kernels, per_device(): pl.pallas_call(sinkhorn_kernel, out_shape=jax.ShapeDtypeStruct((12, 256),...  132 us

profile of v7, /device:TPU:1, one launch (start us, length us, event | category | flops | bytes accessed | tf_op | source)
XLA Modules:
  0.0 135.0 jit_solution(11853870782968255819)
XLA Ops:
  0.0 0.7 copy.8
  0.7 0.8 copy.4.pairs
  1.5 0.0 copy-start
  1.5 1.4 %copy-done = bf16[1,12,256,256]{3,2,1,0:T(8,128)(2,1)S(1)} copy-done((bf16[1,12,256,256]{3,2,1,0:T(8,128)(2,1)S(1)}, bf16[1,12,256,256]{3,2,1,0:T(8,128)(2,1)}, u32[]{:S(2)}) %copy-start) | copy-done | bytes 1572888
  2.9 131.5 %sinkhorn.1 = f32[12,256]{1,0:T(8,128)S(1)} custom-call(bf16[12,256,256]{2,1,0:T(8,128)(2,1)S(1)} %bitcast.6, s32[60,2]{1,0:T(8,128)S(1)} %copy.4.pairs, f32[12,256]{1,0:T(8,128)S(1)} %bitcast.8), custom_call_target="tpu_custom_call" | custom-call | tf_op jit(solution)/shard_map/sinkhorn/pallas_call | solution.py:625
  134.4 0.6 copy.5
Async XLA Ops:
  1.5 1.4 %copy-start = (bf16[1,12,256,256]{3,2,1,0:T(8,128)(2,1)S(1)}, bf16[1,12,256,256]{3,2,1,0:T(8,128)(2,1)}, u32[]{:S(2)}) copy-start(bf16[1,12,256,256]{3,2,1,0:T(8,128)(2,1)} %param.3) | copy-start | bytes 4718596
